TPU v7x, 32 devices: a whole 2x2x4 slice. The times are simulated.
32 devices in a mesh: lon: 8 (over z, core), lat: 4 (over y, x).
Axes of the slice: x: 2, y: 2, z: 4, core: 2. Of those that a mesh axis runs over, the one named last changes fastest.
Arguments:
- innovations: bfloat16 [7, 1024, 16, 128], P(None, ('lon', 'lat')), may hold values from -6 to 6
- fractions: bfloat16 [7, 1024, 2, 128], P(None, ('lon', 'lat')), may hold values from 0 to 1
- cell_index: int32 [7, 1024, 128], P(None, ('lon', 'lat')), may hold values from 0 to 238, as said below
- counts: int32 [7, 1024, 2], P(None, ('lon', 'lat')), may hold values from 0 to 64, as said below
- blocks: int32 [7, 1024, 2], P(None, ('lon', 'lat')), may hold values from 0 to 15
- u_wind: float32 [4, 128, 1024], P(None, 'lat', 'lon'), may hold values from -0.5 to 0.5
- v_wind: float32 [4, 128, 1024], P(None, 'lat', 'lon'), may hold values from -0.5 to 0.5
- channel_mix: float32 [16, 16], replicated
Outputs:
- gradient: float32 [4, 4, 128, 1024], P(None, None, 'lat', 'lon')
Inputs may be any that keep to these rules, and one draw needn't show every extreme that they name: Row and column of a cell inside its tile, cell_index // 16 and cell_index % 16, are each at most 14. `counts`: in every draw some receiving device gets 64 live observations in every tile from every sender.
All inputs are finite; a program needn't handle non-finite values.
Results may differ from a plain program's by a relative error of at most 0.0003.
Values may be sent and summed in bfloat16 or wider, within the bound.
A program may use at most 192 MiB of HBM per device.

v0:
```python
import jax
import jax.numpy as jnp
from jax import lax
from jax.sharding import PartitionSpec as P

VARS = 4
LEV = 4
CH = 16
TILE = 16


KAPPA = 0.125
HIGHEST = lax.Precision.HIGHEST


def with_halo(array, sides, width, wrap):
    for axis, dim in sides:
        count, length = (lax.axis_size(axis), array.shape[dim])
        up = [(i, (i + 1) % count) for i in range(count if wrap else count - 1)]
        down = [(j, i) for i, j in up]
        last = lax.slice_in_dim(array, length - width, length, axis=dim)
        leading = lax.slice_in_dim(array, 0, width, axis=dim)
        before = lax.ppermute(last, axis, up)
        after = lax.ppermute(leading, axis, down)
        array = jnp.concatenate([before, array, after], axis=dim)
    return array


def build_tiles(values, fractions, cell_index, counts):
    targets, channels, width = values.shape
    slot_count = counts.shape[1]
    per_tile = width // slot_count
    within = lax.broadcasted_iota(jnp.int32, (1, 1, per_tile), 2)
    is_live = within < counts[:, :, None]
    frac_y = (
        fractions[:, 0, :].astype(jnp.float32).reshape(targets, slot_count, per_tile)[..., None]
    )
    frac_x = (
        fractions[:, 1, :].astype(jnp.float32).reshape(targets, slot_count, per_tile)[..., None]
    )
    corner = cell_index.reshape(targets, slot_count, per_tile)[..., None]
    position = lax.broadcasted_iota(jnp.int32, (1, 1, 1, TILE * TILE), 3)
    weight = jnp.where(position == corner, (1.0 - frac_y) * (1.0 - frac_x), 0.0)
    weight = weight + jnp.where(position == corner + 1, (1.0 - frac_y) * frac_x, 0.0)
    weight = weight + jnp.where(position == corner + TILE, frac_y * (1.0 - frac_x), 0.0)
    weight = weight + jnp.where(position == corner + TILE + 1, frac_y * frac_x, 0.0)
    weight = jnp.where(is_live[..., None], weight, 0.0)
    innov_f32 = values.reshape(targets, channels, slot_count, per_tile).astype(jnp.float32)
    return jnp.einsum("dcaj,dajp->dacp", innov_f32, weight, precision=HIGHEST)


def build_slot(members):
    return build_tiles(members[0], members[1], members[2], members[3])


def place_tiles(tile_sets, tile_blocks, lat_cells, lon_cells):
    block_rows = lat_cells // TILE
    block_cols = lon_cells // TILE
    block_ids = lax.broadcasted_iota(jnp.int32, (1, 1, 1, block_rows * block_cols), 3)
    onehot = jnp.where(tile_blocks[..., None] == block_ids, 1.0, 0.0).astype(jnp.float32)
    summed = jnp.einsum("sdab,sdacp->scbp", onehot, tile_sets, precision=HIGHEST)
    slot_total = summed.shape[0]
    summed = summed.reshape(slot_total, VARS, LEV, block_rows, block_cols, TILE, TILE)
    summed = jnp.transpose(summed, (0, 1, 2, 3, 5, 4, 6))
    return summed.reshape(slot_total, VARS, LEV, lat_cells, lon_cells)


def shards(innovations, fractions, cell_index, counts, blocks, u_wind, v_wind, channel_mix):
    lat_cells = u_wind.shape[1]
    lon_cells = u_wind.shape[2]
    got_cells, got_counts, got_blocks = (
        lax.all_to_all(cell_index, ("lon", "lat"), split_axis=1, concat_axis=1, tiled=True),
        lax.all_to_all(counts, ("lon", "lat"), split_axis=1, concat_axis=1, tiled=True),
        lax.all_to_all(blocks, ("lon", "lat"), split_axis=1, concat_axis=1, tiled=True),
    )
    got_values, got_fractions = (
        lax.all_to_all(innovations, ("lon", "lat"), split_axis=1, concat_axis=1, tiled=True),
        lax.all_to_all(fractions, ("lon", "lat"), split_axis=1, concat_axis=1, tiled=True),
    )
    tile_sets = lax.map(build_slot, (got_values, got_fractions, got_cells, got_counts))
    forcing = place_tiles(tile_sets, got_blocks, lat_cells, lon_cells)
    slot_total = forcing.shape[0]
    adjoint_field = forcing[slot_total - 1]
    for later in range(slot_total - 2, -1, -1):
        mixed = jnp.einsum(
            "dc,dn->cn",
            channel_mix,
            adjoint_field.reshape(CH, lat_cells * lon_cells),
            precision=HIGHEST,
        )
        mixed = mixed.reshape(VARS, LEV, lat_cells, lon_cells)
        east_flux = u_wind[None] * mixed
        north_flux = v_wind[None] * mixed
        cycle_pad = with_halo(jnp.stack([mixed, east_flux]), (("lon", 4),), 1, True)
        band_pad = with_halo(jnp.stack([mixed, north_flux]), (("lat", 3),), 1, False)
        lon_after = cycle_pad[0, :, :, :, 2:]
        lon_before = cycle_pad[0, :, :, :, :-2]
        east_after = cycle_pad[1, :, :, :, 2:]
        east_before = cycle_pad[1, :, :, :, :-2]
        lat_after = band_pad[0, :, :, 2:, :]
        lat_before = band_pad[0, :, :, :-2, :]
        north_after = band_pad[1, :, :, 2:, :]
        north_before = band_pad[1, :, :, :-2, :]
        spread = lon_after + lon_before + lat_after + lat_before
        carry_term = 0.5 * (east_after - east_before) + 0.5 * (north_after - north_before)
        adjoint_field = (1.0 - 4.0 * KAPPA) * mixed + KAPPA * spread + carry_term + forcing[later]
    return adjoint_field


def solution(mesh):
    in_specs = (
        P(None, ("lon", "lat"), None, None),
        P(None, ("lon", "lat"), None, None),
        P(None, ("lon", "lat"), None),
        P(None, ("lon", "lat"), None),
        P(None, ("lon", "lat"), None),
        P(None, "lat", "lon"),
        P(None, "lat", "lon"),
        P(),
    )
    out_specs = P(None, None, "lat", "lon")
    return jax.shard_map(shards, mesh=mesh, in_specs=in_specs, out_specs=out_specs, check_vma=False)
```

profile of v0, /device:TPU:0, one launch (start us, length us, event | category | flops | bytes accessed | tf_op | source)
XLA Modules:
  0.0 369.8 jit_solution(7796199060638178901)
XLA Ops:
  0.0 1.4 copy.40
  1.4 7.3 %all-to-all-start.1 = ((s32[7,32,2]{0,2,1:T(2,128)}), s32[7,32,2]{0,2,1:T(2,128)S(1)}, u32[]{:S(2)}, u32[]{:S(2)}) async-start(s32[7,32,2]{0,2,1:T(2,128)} %copy.40), calls=%async_computation.1 | async-start | bytes 65536 | tf_op jit(solution)/shard_map/all_to_all | solution.py:73
  8.7 1.4 copy.47
  10.1 5.9 %all-to-all-done.1 = s32[7,32,2]{0,2,1:T(2,128)S(1)} async-done(((s32[7,32,2]{0,2,1:T(2,128)}), s32[7,32,2]{0,2,1:T(2,128)S(1)}, u32[]{:S(2)}, u32[]{:S(2)}) %all-to-all-start.1) | async-done | bytes 1824 | tf_op jit(solution)/shard_map/all_to_all | solution.py:73
  16.0 2.5 all-to-all-start.4
  18.6 1.6 copy.42
  20.2 5.7 %all-to-all-done.4 = s32[7,32,2]{0,2,1:T(2,128)S(1)} async-done(((s32[7,32,2]{0,2,1:T(2,128)}), s32[7,32,2]{0,2,1:T(2,128)S(1)}, u32[]{:S(2)}, u32[]{:S(2)}) %all-to-all-start.4) | async-done | bytes 1824 | tf_op jit(solution)/shard_map/all_to_all | solution.py:74
  25.9 2.6 all-to-all-start.3
  28.4 1.6 copy.41
  30.1 6.5 %all-to-all-done.3 = bf16[7,32,2,128]{3,2,0,1:T(2,128)(2,1)S(1)} async-done(((bf16[7,32,2,128]{3,2,0,1:T(2,128)(2,1)}), bf16[7,32,2,128]{3,2,0,1:T(2,128)(2,1)S(1)}, u32[]{:S(2)}, u32[]{:S(2)}) %all-to-all-start.3) | async-done | bytes 114720 | tf_op jit(solution)/shard_map/all_to_all | solution.py:78
  36.6 2.6 all-to-all-start.2
  39.2 2.4 copy.39
  41.5 6.1 %all-to-all-done.2 = s32[7,32,128]{2,0,1:T(8,128)S(1)} async-done(((s32[7,32,128]{2,0,1:T(8,128)}), s32[7,32,128]{2,0,1:T(8,128)S(1)}, u32[]{:S(2)}, u32[]{:S(2)}) %all-to-all-start.2) | async-done | bytes 114720 | tf_op jit(solution)/shard_map/all_to_all | solution.py:72
  47.6 2.6 all-to-all-start
  50.4 23.7 %all-to-all-done = bf16[7,32,16,128]{3,2,0,1:T(8,128)(2,1)S(1)} async-done(((bf16[7,32,16,128]{3,2,0,1:T(8,128)(2,1)}), bf16[7,32,16,128]{3,2,0,1:T(8,128)(2,1)S(1)}, u32[]{:S(2)}, u32[]{:S(2)}) %all-to-all-start) | async-done | bytes 917536 | tf_op jit(solution)/shard_map/all_to_all | solution.py:77
  74.1 100.5 %while.12 = (s32[]{:T(128)}, f32[7,32,2,16,256]{4,1,2,3,0:T(8,128)}, bf16[7,32,16,128]{3,2,0,1:T(8,128)(2,1)S(1)}, s32[7,32,2]{1,2,0:T(2,128)S(1)}, s32[7,32,128...) while((s32[]{:T(128)}, f32[7,32,2,16,256]{4,1,2,3,0:T(8,128)}, ...), condition=%wide.region_1.2_spmd, body=%wide.region_0.1_spmd.sunk | while | flops 213958656 | bytes 4351337 | solution.py:80
  74.9 11.9 %fusion.132 = f32[1,32,2,16,256]{4,3,2,1,0:T(8,128)S(1)} fusion(f32[32,2,64]{2,1,0:T(2,128)S(1)} %get-tuple-element.207, s32[32,2,64]{2,1,0:T(2,128)S(1)} %get-tuple-element.208, f32[32,2,64]{2,1,0:T(2,128)S(1)} %get-tuple-element.209, s32[32,2,64]{2,1,0:T(2,128)S(1)} %get-tuple-element.210, f32[32,2,64]{2,1,0:T(2,128)S(1)} %get-tuple-element.211, ...), kind=kOutput, calls=%fused_computation.23.clone.1 | convolution fusion | flops 213909504 | bytes 1314816 | tf_op jit(solution)/shard_map/while/body/eval_jaxpr/dcaj,dajp->dacp/dot_general | solution.py:49
  86.9 1.6 copy_dynamic-update-slice_fusion.2
  89.3 11.9 %fusion.132 = f32[1,32,2,16,256]{4,3,2,1,0:T(8,128)S(1)} fusion(f32[32,2,64]{2,1,0:T(2,128)S(1)} %get-tuple-element.207, s32[32,2,64]{2,1,0:T(2,128)S(1)} %get-tuple-element.208, f32[32,2,64]{2,1,0:T(2,128)S(1)} %get-tuple-element.209, s32[32,2,64]{2,1,0:T(2,128)S(1)} %get-tuple-element.210, f32[32,2,64]{2,1,0:T(2,128)S(1)} %get-tuple-element.211, ...), kind=kOutput, calls=%fused_computation.23.clone.1 | convolution fusion | flops 213909504 | bytes 1314816 | tf_op jit(solution)/shard_map/while/body/eval_jaxpr/dcaj,dajp->dacp/dot_general | solution.py:49
  101.3 1.6 copy_dynamic-update-slice_fusion.2
  103.7 11.9 %fusion.132 = f32[1,32,2,16,256]{4,3,2,1,0:T(8,128)S(1)} fusion(f32[32,2,64]{2,1,0:T(2,128)S(1)} %get-tuple-element.207, s32[32,2,64]{2,1,0:T(2,128)S(1)} %get-tuple-element.208, f32[32,2,64]{2,1,0:T(2,128)S(1)} %get-tuple-element.209, s32[32,2,64]{2,1,0:T(2,128)S(1)} %get-tuple-element.210, f32[32,2,64]{2,1,0:T(2,128)S(1)} %get-tuple-element.211, ...), kind=kOutput, calls=%fused_computation.23.clone.1 | convolution fusion | flops 213909504 | bytes 1314816 | tf_op jit(solution)/shard_map/while/body/eval_jaxpr/dcaj,dajp->dacp/dot_general | solution.py:49
  115.6 1.6 copy_dynamic-update-slice_fusion.2
  118.0 11.9 %fusion.132 = f32[1,32,2,16,256]{4,3,2,1,0:T(8,128)S(1)} fusion(f32[32,2,64]{2,1,0:T(2,128)S(1)} %get-tuple-element.207, s32[32,2,64]{2,1,0:T(2,128)S(1)} %get-tuple-element.208, f32[32,2,64]{2,1,0:T(2,128)S(1)} %get-tuple-element.209, s32[32,2,64]{2,1,0:T(2,128)S(1)} %get-tuple-element.210, f32[32,2,64]{2,1,0:T(2,128)S(1)} %get-tuple-element.211, ...), kind=kOutput, calls=%fused_computation.23.clone.1 | convolution fusion | flops 213909504 | bytes 1314816 | tf_op jit(solution)/shard_map/while/body/eval_jaxpr/dcaj,dajp->dacp/dot_general | solution.py:49
  130.0 1.6 copy_dynamic-update-slice_fusion.2
  132.4 11.9 %fusion.132 = f32[1,32,2,16,256]{4,3,2,1,0:T(8,128)S(1)} fusion(f32[32,2,64]{2,1,0:T(2,128)S(1)} %get-tuple-element.207, s32[32,2,64]{2,1,0:T(2,128)S(1)} %get-tuple-element.208, f32[32,2,64]{2,1,0:T(2,128)S(1)} %get-tuple-element.209, s32[32,2,64]{2,1,0:T(2,128)S(1)} %get-tuple-element.210, f32[32,2,64]{2,1,0:T(2,128)S(1)} %get-tuple-element.211, ...), kind=kOutput, calls=%fused_computation.23.clone.1 | convolution fusion | flops 213909504 | bytes 1314816 | tf_op jit(solution)/shard_map/while/body/eval_jaxpr/dcaj,dajp->dacp/dot_general | solution.py:49
  144.3 1.6 copy_dynamic-update-slice_fusion.2
  146.7 11.9 %fusion.132 = f32[1,32,2,16,256]{4,3,2,1,0:T(8,128)S(1)} fusion(f32[32,2,64]{2,1,0:T(2,128)S(1)} %get-tuple-element.207, s32[32,2,64]{2,1,0:T(2,128)S(1)} %get-tuple-element.208, f32[32,2,64]{2,1,0:T(2,128)S(1)} %get-tuple-element.209, s32[32,2,64]{2,1,0:T(2,128)S(1)} %get-tuple-element.210, f32[32,2,64]{2,1,0:T(2,128)S(1)} %get-tuple-element.211, ...), kind=kOutput, calls=%fused_computation.23.clone.1 | convolution fusion | flops 213909504 | bytes 1314816 | tf_op jit(solution)/shard_map/while/body/eval_jaxpr/dcaj,dajp->dacp/dot_general | solution.py:49
  158.6 1.6 copy_dynamic-update-slice_fusion.2
  161.1 11.9 %fusion.132 = f32[1,32,2,16,256]{4,3,2,1,0:T(8,128)S(1)} fusion(f32[32,2,64]{2,1,0:T(2,128)S(1)} %get-tuple-element.207, s32[32,2,64]{2,1,0:T(2,128)S(1)} %get-tuple-element.208, f32[32,2,64]{2,1,0:T(2,128)S(1)} %get-tuple-element.209, s32[32,2,64]{2,1,0:T(2,128)S(1)} %get-tuple-element.210, f32[32,2,64]{2,1,0:T(2,128)S(1)} %get-tuple-element.211, ...), kind=kOutput, calls=%fused_computation.23.clone.1 | convolution fusion | flops 213909504 | bytes 1314816 | tf_op jit(solution)/shard_map/while/body/eval_jaxpr/dcaj,dajp->dacp/dot_general | solution.py:49
  173.0 1.6 copy_dynamic-update-slice_fusion.2
  174.6 6.1 %convolution_bitcast_fusion = f32[7,16,16,256]{3,2,1,0:T(8,128)S(1)} fusion(f32[7,32,2,16,256]{4,1,2,3,0:T(8,128)} %get-tuple-element.82, s32[7,32,2]{1,2,0:T(2,128)S(1)} %copy.48), kind=kOutput, calls=%fused_computation.43 | convolution fusion | flops 352335872 | bytes 9176832 | tf_op jit(solution)/shard_map/sdab,sdacp->scbp/dot_general | solution.py:61
  180.8 8.1 %reshape.386 = f32[7,4,4,2,8,16,16]{6,5,4,3,2,1,0:T(8,128)} reshape(f32[7,16,16,256]{3,2,1,0:T(8,128)S(1)} %convolution_bitcast_fusion) | data formatting | bytes 3670016 | tf_op jit(solution)/shard_map/reshape | solution.py:63
  188.8 17.7 %copy.121 = f32[7,4,4,2,8,16,16]{6,4,5,3,2,1,0:T(8,128)} copy(f32[7,4,4,2,8,16,16]{6,5,4,3,2,1,0:T(8,128)} %reshape.386) | data formatting | bytes 3670016 | tf_op jit(solution)/shard_map/reshape | solution.py:63
  206.5 10.6 %fusion.115 = (f32[1,4,4,2,16,8,16]{6,5,4,3,2,1,0:T(8,128)}, f32[1,4,4,2,16,8,16]{6,5,4,3,2,1,0:T(8,128)}, f32[1,4,4,2,16,8,16]{6,5,4,3,2,1,0:T(8,128)S(1)}, f32...) fusion(f32[7,4,4,2,16,8,16]{6,5,4,3,2,1,0:T(8,128)} %bitcast.196), kind=kLoop, calls=%fused_computation.254 | loop fusion | bytes 3670016 | tf_op jit(solution)/shard_map/slice | solution.py:83
  217.2 3.1 reshape_squeeze.3
  222.2 4.5 %collective-permute-start.3 = (f32[2,4,4,1,128]{4,3,2,1,0:T(1,128)S(1)}, f32[2,4,4,1,128]{4,3,2,1,0:T(1,128)S(1)}, u32[]{:S(2)}, u32[]{:S(2)}) collective-permute-start(f32[2,4,4,1,128]{4,3,2,1,0:T(1,128)S(1)} %get-tuple-element.146), channel_id=1, source_target_pairs={{0,1},{1,2},{2,3},{4,5},{5,6},{6,7},{8,9},{9,10},{10,11},{12,13},{... | collective-permute-start | bytes 49160 | tf_op jit(solution)/shard_map/ppermute | solution.py:23
  228.5 3.8 %squeeze.27 = f32[16,4096]{1,0:T(8,128)} reshape(f32[1,4,4,2,16,8,16]{6,5,4,3,2,1,0:T(8,128)} %get-tuple-element.122) | data formatting | bytes 524288 | tf_op jit(solution)/shard_map/squeeze | solution.py:106
  232.3 7.3 %collective-permute-done = f32[2,4,4,32,1]{4,3,2,1,0:T(8,128)} collective-permute-done((f32[2,4,4,32,1]{4,3,2,1,0:T(8,128)}, f32[2,4,4,32,1]{4,3,2,1,0:T(8,128)}, u32[]{:S(2)}, u32[]{:S(2)}) %collective-permute-start) | collective-permute-done | bytes 4128 | tf_op jit(solution)/shard_map/ppermute | solution.py:24
  239.6 3.0 collective-permute-done.1
  242.7 1.3 fusion.90
  247.5 4.5 %collective-permute-start.7 = (f32[2,4,4,1,128]{4,3,2,1,0:T(1,128)S(1)}, f32[2,4,4,1,128]{4,3,2,1,0:T(1,128)S(1)}, u32[]{:S(2)}, u32[]{:S(2)}) collective-permute-start(f32[2,4,4,1,128]{4,3,2,1,0:T(1,128)S(1)} %get-tuple-element.142), channel_id=1, source_target_pairs={{0,1},{1,2},{2,3},{4,5},{5,6},{6,7},{8,9},{9,10},{10,11},{12,13},{... | collective-permute-start | bytes 49160 | tf_op jit(solution)/shard_map/ppermute | solution.py:23
  254.5 3.8 %squeeze.28 = f32[16,4096]{1,0:T(8,128)} reshape(f32[1,4,4,2,16,8,16]{6,5,4,3,2,1,0:T(8,128)} %get-tuple-element.121) | data formatting | bytes 524288 | tf_op jit(solution)/shard_map/squeeze | solution.py:106
  258.4 8.1 %collective-permute-done.4 = f32[2,4,4,32,1]{4,3,2,1,0:T(8,128)} collective-permute-done((f32[2,4,4,32,1]{4,3,2,1,0:T(8,128)}, f32[2,4,4,32,1]{4,3,2,1,0:T(8,128)}, u32[]{:S(2)}, u32[]{:S(2)}) %collective-permute-start.4) | collective-permute-done | bytes 4128 | tf_op jit(solution)/shard_map/ppermute | solution.py:24
  272.6 4.5 %collective-permute-start.11 = (f32[2,4,4,1,128]{4,3,2,1,0:T(1,128)S(1)}, f32[2,4,4,1,128]{4,3,2,1,0:T(1,128)S(1)}, u32[]{:S(2)}, u32[]{:S(2)}) collective-permute-start(f32[2,4,4,1,128]{4,3,2,1,0:T(1,128)S(1)} %get-tuple-element.138), channel_id=1, source_target_pairs={{0,1},{1,2},{2,3},{4,5},{5,6},{6,7},{8,9},{9,10},{10,11},{12,13},{... | collective-permute-start | bytes 49160 | tf_op jit(solution)/shard_map/ppermute | solution.py:23
  278.3 1.9 collective-permute-start.8
  280.3 3.8 %squeeze.29 = f32[16,4096]{1,0:T(8,128)} reshape(f32[1,4,4,2,16,8,16]{6,5,4,3,2,1,0:T(8,128)} %get-tuple-element.120) | data formatting | bytes 524288 | tf_op jit(solution)/shard_map/squeeze | solution.py:106
  284.1 7.0 %collective-permute-done.8 = f32[2,4,4,32,1]{4,3,2,1,0:T(8,128)} collective-permute-done((f32[2,4,4,32,1]{4,3,2,1,0:T(8,128)}, f32[2,4,4,32,1]{4,3,2,1,0:T(8,128)}, u32[]{:S(2)}, u32[]{:S(2)}) %collective-permute-start.8) | collective-permute-done | bytes 4128 | tf_op jit(solution)/shard_map/ppermute | solution.py:24
  296.6 5.8 %collective-permute-start.15 = (f32[2,4,4,1,128]{4,3,2,1,0:T(1,128)}, f32[2,4,4,1,128]{4,3,2,1,0:T(1,128)}, u32[]{:S(2)}, u32[]{:S(2)}) collective-permute-start(f32[2,4,4,1,128]{4,3,2,1,0:T(1,128)} %get-tuple-element.134), channel_id=1, source_target_pairs={{0,1},{1,2},{2,3},{4,5},{5,6},{6,7},{8,9},{9,10},{10,11},{12,13},{... | collective-permute-start | bytes 49160 | tf_op jit(solution)/shard_map/ppermute | solution.py:23
  303.5 3.4 collective-permute-start.12
  306.9 3.1 squeeze.30
  310.1 7.7 %collective-permute-done.12 = f32[2,4,4,32,1]{4,3,2,1,0:T(8,128)} collective-permute-done((f32[2,4,4,32,1]{4,3,2,1,0:T(8,128)}, f32[2,4,4,32,1]{4,3,2,1,0:T(8,128)}, u32[]{:S(2)}, u32[]{:S(2)}) %collective-permute-start.12) | collective-permute-done | bytes 4128 | tf_op jit(solution)/shard_map/ppermute | solution.py:24
  317.8 1.4 fusion.75
  319.2 1.4 fusion.73
  320.5 1.7 fusion.37
  324.3 5.2 %collective-permute-start.19 = (f32[2,4,4,1,128]{4,3,2,1,0:T(1,128)}, f32[2,4,4,1,128]{4,3,2,1,0:T(1,128)}, u32[]{:S(2)}, u32[]{:S(2)}) collective-permute-start(f32[2,4,4,1,128]{4,3,2,1,0:T(1,128)} %get-tuple-element.130), channel_id=1, source_target_pairs={{0,1},{1,2},{2,3},{4,5},{5,6},{6,7},{8,9},{9,10},{10,11},{12,13},{... | collective-permute-start | bytes 49160 | tf_op jit(solution)/shard_map/ppermute | solution.py:23
  330.6 3.4 collective-permute-start.16
  334.0 2.8 squeeze.32
  336.8 1.6 squeeze.31
  338.3 6.5 %collective-permute-done.16 = f32[2,4,4,32,1]{4,3,2,1,0:T(8,128)} collective-permute-done((f32[2,4,4,32,1]{4,3,2,1,0:T(8,128)}, f32[2,4,4,32,1]{4,3,2,1,0:T(8,128)}, u32[]{:S(2)}, u32[]{:S(2)}) %collective-permute-start.16) | collective-permute-done | bytes 4128 | tf_op jit(solution)/shard_map/ppermute | solution.py:24
  344.9 1.4 fusion.70
  346.3 1.4 fusion.68
  349.8 4.6 %collective-permute-start.23 = (f32[2,4,4,1,128]{4,3,2,1,0:T(1,128)S(1)}, f32[2,4,4,1,128]{4,3,2,1,0:T(1,128)S(1)}, u32[]{:S(2)}, u32[]{:S(2)}) collective-permute-start(f32[2,4,4,1,128]{4,3,2,1,0:T(1,128)S(1)} %get-tuple-element.126), channel_id=1, source_target_pairs={{0,1},{1,2},{2,3},{4,5},{5,6},{6,7},{8,9},{9,10},{10,11},{12,13},{... | collective-permute-start | bytes 49160 | tf_op jit(solution)/shard_map/ppermute | solution.py:23
  354.6 3.4 collective-permute-start.20
  358.2 10.4 %collective-permute-done.20 = f32[2,4,4,32,1]{4,3,2,1,0:T(8,128)S(1)} collective-permute-done((f32[2,4,4,32,1]{4,3,2,1,0:T(8,128)S(1)}, f32[2,4,4,32,1]{4,3,2,1,0:T(8,128)S(1)}, u32[]{:S(2)}, u32[]{:S(2)}) %collective-permute-start.20) | collective-permute-done | bytes 4128 | tf_op jit(solution)/shard_map/ppermute | solution.py:24
  (185 shorter events, 35.6 us)
Async XLA Ops:
  0.0 220.3 %copy-start = (f32[16,16]{1,0:T(8,128)S(1)}, f32[16,16]{1,0:T(8,128)}, u32[]{:S(2)}) copy-start(f32[16,16]{1,0:T(8,128)} %param.17) | copy-start | bytes 3076
  1.4 14.6 %all-to-all-start.1 = ((s32[7,32,2]{0,2,1:T(2,128)}), s32[7,32,2]{0,2,1:T(2,128)S(1)}, u32[]{:S(2)}, u32[]{:S(2)}) async-start(s32[7,32,2]{0,2,1:T(2,128)} %copy.40), calls=%async_computation.1 | async-start | bytes 65536 | tf_op jit(solution)/shard_map/all_to_all | solution.py:73
  16.0 9.9 %all-to-all-start.4 = ((s32[7,32,2]{0,2,1:T(2,128)}), s32[7,32,2]{0,2,1:T(2,128)S(1)}, u32[]{:S(2)}, u32[]{:S(2)}) async-start(s32[7,32,2]{0,2,1:T(2,128)} %copy.47), calls=%async_computation.4 | async-start | bytes 65536 | tf_op jit(solution)/shard_map/all_to_all | solution.py:74
  25.9 10.7 %all-to-all-start.3 = ((bf16[7,32,2,128]{3,2,0,1:T(2,128)(2,1)}), bf16[7,32,2,128]{3,2,0,1:T(2,128)(2,1)S(1)}, u32[]{:S(2)}, u32[]{:S(2)}) async-start(bf16[7,32,2,128]{3,2,0,1:T(2,128)(2,1)} %copy.42), calls=%async_computation.3 | async-start | bytes 229376 | tf_op jit(solution)/shard_map/all_to_all | solution.py:78
  36.6 11.0 %all-to-all-start.2 = ((s32[7,32,128]{2,0,1:T(8,128)}), s32[7,32,128]{2,0,1:T(8,128)S(1)}, u32[]{:S(2)}, u32[]{:S(2)}) async-start(s32[7,32,128]{2,0,1:T(8,128)} %copy.41), calls=%async_computation.2 | async-start | bytes 262144 | tf_op jit(solution)/shard_map/all_to_all | solution.py:72
  47.6 26.5 %all-to-all-start = ((bf16[7,32,16,128]{3,2,0,1:T(8,128)(2,1)}), bf16[7,32,16,128]{3,2,0,1:T(8,128)(2,1)S(1)}, u32[]{:S(2)}, u32[]{:S(2)}) async-start(bf16[7,32,16,128]{3,2,0,1:T(8,128)(2,1)} %copy.39), calls=%async_computation | async-start | bytes 1835008 | tf_op jit(solution)/shard_map/all_to_all | solution.py:77
  206.5 14.3 %copy-start.1 = (f32[4,32,128]{2,1,0:T(8,128)S(1)}, f32[4,32,128]{2,1,0:T(8,128)}, u32[]{:S(2)}) copy-start(f32[4,32,128]{2,1,0:T(8,128)} %param.15) | copy-start | bytes 196612
  206.5 14.3 %copy-start.2 = (f32[4,32,128]{2,1,0:T(8,128)S(1)}, f32[4,32,128]{2,1,0:T(8,128)}, u32[]{:S(2)}) copy-start(f32[4,32,128]{2,1,0:T(8,128)} %param.16) | copy-start | bytes 196612
  220.9 21.7 %collective-permute-start.2 = (f32[2,4,4,1,128]{4,3,2,1,0:T(1,128)S(1)}, f32[2,4,4,1,128]{4,3,2,1,0:T(1,128)S(1)}, u32[]{:S(2)}, u32[]{:S(2)}) collective-permute-start(f32[2,4,4,1,128]{4,3,2,1,0:T(1,128)S(1)} %get-tuple-element.145), channel_id=1, source_target_pairs={{1,0},{2,1},{3,2},{5,4},{6,5},{7,6},{9,8},{10,9},{11,10},{13,12},{... | collective-permute-start | bytes 49160 | tf_op jit(solution)/shard_map/ppermute | solution.py:24
  222.2 20.4 %collective-permute-start.3 = (f32[2,4,4,1,128]{4,3,2,1,0:T(1,128)S(1)}, f32[2,4,4,1,128]{4,3,2,1,0:T(1,128)S(1)}, u32[]{:S(2)}, u32[]{:S(2)}) collective-permute-start(f32[2,4,4,1,128]{4,3,2,1,0:T(1,128)S(1)} %get-tuple-element.146), channel_id=1, source_target_pairs={{0,1},{1,2},{2,3},{4,5},{5,6},{6,7},{8,9},{9,10},{10,11},{12,13},{... | collective-permute-start | bytes 49160 | tf_op jit(solution)/shard_map/ppermute | solution.py:23
  228.0 11.7 %collective-permute-start = (f32[2,4,4,32,1]{4,3,2,1,0:T(8,128)}, f32[2,4,4,32,1]{4,3,2,1,0:T(8,128)}, u32[]{:S(2)}, u32[]{:S(2)}) collective-permute-start(f32[2,4,4,32,1]{4,3,2,1,0:T(8,128)} %get-tuple-element.143), channel_id=1, source_target_pairs={{4,0},{8,4},{12,8},{16,12},{20,16},{24,20},{28,24},{0,28},{5,1},{9... | collective-permute-start | bytes 12296 | tf_op jit(solution)/shard_map/ppermute | solution.py:24
  228.0 14.7 %collective-permute-start.1 = (f32[2,4,4,32,1]{4,3,2,1,0:T(8,128)}, f32[2,4,4,32,1]{4,3,2,1,0:T(8,128)}, u32[]{:S(2)}, u32[]{:S(2)}) collective-permute-start(f32[2,4,4,32,1]{4,3,2,1,0:T(8,128)} %get-tuple-element.144), channel_id=1, source_target_pairs={{0,4},{4,8},{8,12},{12,16},{16,20},{20,24},{24,28},{28,0},{1,5},{5... | collective-permute-start | bytes 12296 | tf_op jit(solution)/shard_map/ppermute | solution.py:23
  232.3 13.0 %copy-start.4 = (f32[16,4096]{1,0:T(8,128)S(1)}, f32[16,4096]{1,0:T(8,128)}, u32[]{:S(2)}) copy-start(f32[16,4096]{1,0:T(8,128)} %squeeze.27) | copy-start | bytes 786436
  246.2 21.5 %collective-permute-start.6 = (f32[2,4,4,1,128]{4,3,2,1,0:T(1,128)S(1)}, f32[2,4,4,1,128]{4,3,2,1,0:T(1,128)S(1)}, u32[]{:S(2)}, u32[]{:S(2)}) collective-permute-start(f32[2,4,4,1,128]{4,3,2,1,0:T(1,128)S(1)} %get-tuple-element.141), channel_id=1, source_target_pairs={{1,0},{2,1},{3,2},{5,4},{6,5},{7,6},{9,8},{10,9},{11,10},{13,12},{... | collective-permute-start | bytes 49160 | tf_op jit(solution)/shard_map/ppermute | solution.py:24
  247.5 20.2 %collective-permute-start.7 = (f32[2,4,4,1,128]{4,3,2,1,0:T(1,128)S(1)}, f32[2,4,4,1,128]{4,3,2,1,0:T(1,128)S(1)}, u32[]{:S(2)}, u32[]{:S(2)}) collective-permute-start(f32[2,4,4,1,128]{4,3,2,1,0:T(1,128)S(1)} %get-tuple-element.142), channel_id=1, source_target_pairs={{0,1},{1,2},{2,3},{4,5},{5,6},{6,7},{8,9},{9,10},{10,11},{12,13},{... | collective-permute-start | bytes 49160 | tf_op jit(solution)/shard_map/ppermute | solution.py:23
  253.3 13.2 %collective-permute-start.4 = (f32[2,4,4,32,1]{4,3,2,1,0:T(8,128)}, f32[2,4,4,32,1]{4,3,2,1,0:T(8,128)}, u32[]{:S(2)}, u32[]{:S(2)}) collective-permute-start(f32[2,4,4,32,1]{4,3,2,1,0:T(8,128)} %get-tuple-element.139), channel_id=1, source_target_pairs={{4,0},{8,4},{12,8},{16,12},{20,16},{24,20},{28,24},{0,28},{5,1},{9... | collective-permute-start | bytes 12296 | tf_op jit(solution)/shard_map/ppermute | solution.py:24
  254.5 13.2 %collective-permute-start.5 = (f32[2,4,4,32,1]{4,3,2,1,0:T(8,128)}, f32[2,4,4,32,1]{4,3,2,1,0:T(8,128)}, u32[]{:S(2)}, u32[]{:S(2)}) collective-permute-start(f32[2,4,4,32,1]{4,3,2,1,0:T(8,128)} %get-tuple-element.140), channel_id=1, source_target_pairs={{0,4},{4,8},{8,12},{12,16},{16,20},{20,24},{24,28},{28,0},{1,5},{5... | collective-permute-start | bytes 12296 | tf_op jit(solution)/shard_map/ppermute | solution.py:23
  258.4 12.0 %copy-start.5 = (f32[16,4096]{1,0:T(8,128)S(1)}, f32[16,4096]{1,0:T(8,128)}, u32[]{:S(2)}) copy-start(f32[16,4096]{1,0:T(8,128)} %squeeze.28) | copy-start | bytes 786436
  271.3 19.9 %collective-permute-start.10 = (f32[2,4,4,1,128]{4,3,2,1,0:T(1,128)S(1)}, f32[2,4,4,1,128]{4,3,2,1,0:T(1,128)S(1)}, u32[]{:S(2)}, u32[]{:S(2)}) collective-permute-start(f32[2,4,4,1,128]{4,3,2,1,0:T(1,128)S(1)} %get-tuple-element.137), channel_id=1, source_target_pairs={{1,0},{2,1},{3,2},{5,4},{6,5},{7,6},{9,8},{10,9},{11,10},{13,12},{... | collective-permute-start | bytes 49160 | tf_op jit(solution)/shard_map/ppermute | solution.py:24
  272.6 18.6 %collective-permute-start.11 = (f32[2,4,4,1,128]{4,3,2,1,0:T(1,128)S(1)}, f32[2,4,4,1,128]{4,3,2,1,0:T(1,128)S(1)}, u32[]{:S(2)}, u32[]{:S(2)}) collective-permute-start(f32[2,4,4,1,128]{4,3,2,1,0:T(1,128)S(1)} %get-tuple-element.138), channel_id=1, source_target_pairs={{0,1},{1,2},{2,3},{4,5},{5,6},{6,7},{8,9},{9,10},{10,11},{12,13},{... | collective-permute-start | bytes 49160 | tf_op jit(solution)/shard_map/ppermute | solution.py:23
  278.3 12.8 %collective-permute-start.8 = (f32[2,4,4,32,1]{4,3,2,1,0:T(8,128)}, f32[2,4,4,32,1]{4,3,2,1,0:T(8,128)}, u32[]{:S(2)}, u32[]{:S(2)}) collective-permute-start(f32[2,4,4,32,1]{4,3,2,1,0:T(8,128)} %get-tuple-element.135), channel_id=1, source_target_pairs={{4,0},{8,4},{12,8},{16,12},{20,16},{24,20},{28,24},{0,28},{5,1},{9... | collective-permute-start | bytes 12296 | tf_op jit(solution)/shard_map/ppermute | solution.py:24
  280.3 10.9 %collective-permute-start.9 = (f32[2,4,4,32,1]{4,3,2,1,0:T(8,128)}, f32[2,4,4,32,1]{4,3,2,1,0:T(8,128)}, u32[]{:S(2)}, u32[]{:S(2)}) collective-permute-start(f32[2,4,4,32,1]{4,3,2,1,0:T(8,128)} %get-tuple-element.136), channel_id=1, source_target_pairs={{0,4},{4,8},{8,12},{12,16},{16,20},{20,24},{24,28},{28,0},{1,5},{5... | collective-permute-start | bytes 12296 | tf_op jit(solution)/shard_map/ppermute | solution.py:23
  284.1 9.7 %copy-start.6 = (f32[16,4096]{1,0:T(8,128)S(1)}, f32[16,4096]{1,0:T(8,128)}, u32[]{:S(2)}) copy-start(f32[16,4096]{1,0:T(8,128)} %squeeze.29) | copy-start | bytes 786436
  294.5 26.0 %copy-start.3 = (f32[4096,16]{0,1:T(8,128)}, f32[4096,16]{0,1:T(8,128)S(1)}, u32[]{:S(2)}) copy-start(f32[4096,16]{0,1:T(8,128)S(1)} %fusion.42) | copy-start | bytes 786436
  295.3 22.5 %collective-permute-start.14 = (f32[2,4,4,1,128]{4,3,2,1,0:T(1,128)}, f32[2,4,4,1,128]{4,3,2,1,0:T(1,128)}, u32[]{:S(2)}, u32[]{:S(2)}) collective-permute-start(f32[2,4,4,1,128]{4,3,2,1,0:T(1,128)} %get-tuple-element.133), channel_id=1, source_target_pairs={{1,0},{2,1},{3,2},{5,4},{6,5},{7,6},{9,8},{10,9},{11,10},{13,12},{... | collective-permute-start | bytes 49160 | tf_op jit(solution)/shard_map/ppermute | solution.py:24
  296.6 21.2 %collective-permute-start.15 = (f32[2,4,4,1,128]{4,3,2,1,0:T(1,128)}, f32[2,4,4,1,128]{4,3,2,1,0:T(1,128)}, u32[]{:S(2)}, u32[]{:S(2)}) collective-permute-start(f32[2,4,4,1,128]{4,3,2,1,0:T(1,128)} %get-tuple-element.134), channel_id=1, source_target_pairs={{0,1},{1,2},{2,3},{4,5},{5,6},{6,7},{8,9},{9,10},{10,11},{12,13},{... | collective-permute-start | bytes 49160 | tf_op jit(solution)/shard_map/ppermute | solution.py:23
  303.5 14.2 %collective-permute-start.12 = (f32[2,4,4,32,1]{4,3,2,1,0:T(8,128)}, f32[2,4,4,32,1]{4,3,2,1,0:T(8,128)}, u32[]{:S(2)}, u32[]{:S(2)}) collective-permute-start(f32[2,4,4,32,1]{4,3,2,1,0:T(8,128)} %get-tuple-element.131), channel_id=1, source_target_pairs={{4,0},{8,4},{12,8},{16,12},{20,16},{24,20},{28,24},{0,28},{5,1},{9... | collective-permute-start | bytes 12296 | tf_op jit(solution)/shard_map/ppermute | solution.py:24
  306.9 10.9 %collective-permute-start.13 = (f32[2,4,4,32,1]{4,3,2,1,0:T(8,128)}, f32[2,4,4,32,1]{4,3,2,1,0:T(8,128)}, u32[]{:S(2)}, u32[]{:S(2)}) collective-permute-start(f32[2,4,4,32,1]{4,3,2,1,0:T(8,128)} %get-tuple-element.132), channel_id=1, source_target_pairs={{0,4},{4,8},{8,12},{12,16},{16,20},{20,24},{24,28},{28,0},{1,5},{5... | collective-permute-start | bytes 12296 | tf_op jit(solution)/shard_map/ppermute | solution.py:23
  323.0 21.9 %collective-permute-start.18 = (f32[2,4,4,1,128]{4,3,2,1,0:T(1,128)}, f32[2,4,4,1,128]{4,3,2,1,0:T(1,128)}, u32[]{:S(2)}, u32[]{:S(2)}) collective-permute-start(f32[2,4,4,1,128]{4,3,2,1,0:T(1,128)} %get-tuple-element.129), channel_id=1, source_target_pairs={{1,0},{2,1},{3,2},{5,4},{6,5},{7,6},{9,8},{10,9},{11,10},{13,12},{... | collective-permute-start | bytes 49160 | tf_op jit(solution)/shard_map/ppermute | solution.py:24
  324.3 20.6 %collective-permute-start.19 = (f32[2,4,4,1,128]{4,3,2,1,0:T(1,128)}, f32[2,4,4,1,128]{4,3,2,1,0:T(1,128)}, u32[]{:S(2)}, u32[]{:S(2)}) collective-permute-start(f32[2,4,4,1,128]{4,3,2,1,0:T(1,128)} %get-tuple-element.130), channel_id=1, source_target_pairs={{0,1},{1,2},{2,3},{4,5},{5,6},{6,7},{8,9},{9,10},{10,11},{12,13},{... | collective-permute-start | bytes 49160 | tf_op jit(solution)/shard_map/ppermute | solution.py:23
  330.6 14.2 %collective-permute-start.16 = (f32[2,4,4,32,1]{4,3,2,1,0:T(8,128)}, f32[2,4,4,32,1]{4,3,2,1,0:T(8,128)}, u32[]{:S(2)}, u32[]{:S(2)}) collective-permute-start(f32[2,4,4,32,1]{4,3,2,1,0:T(8,128)} %get-tuple-element.127), channel_id=1, source_target_pairs={{4,0},{8,4},{12,8},{16,12},{20,16},{24,20},{28,24},{0,28},{5,1},{9... | collective-permute-start | bytes 12296 | tf_op jit(solution)/shard_map/ppermute | solution.py:24
  334.0 10.9 %collective-permute-start.17 = (f32[2,4,4,32,1]{4,3,2,1,0:T(8,128)}, f32[2,4,4,32,1]{4,3,2,1,0:T(8,128)}, u32[]{:S(2)}, u32[]{:S(2)}) collective-permute-start(f32[2,4,4,32,1]{4,3,2,1,0:T(8,128)} %get-tuple-element.128), channel_id=1, source_target_pairs={{0,4},{4,8},{8,12},{12,16},{16,20},{20,24},{24,28},{28,0},{1,5},{5... | collective-permute-start | bytes 12296 | tf_op jit(solution)/shard_map/ppermute | solution.py:23
  346.2 22.4 %copy-start.7 = (f32[4,4,32,128]{3,2,1,0:T(8,128)S(1)}, f32[4,4,32,128]{3,2,1,0:T(8,128)}, u32[]{:S(2)}) copy-start(f32[4,4,32,128]{3,2,1,0:T(8,128)} %squeeze.32) | copy-start | bytes 786436
  348.5 20.1 %collective-permute-start.22 = (f32[2,4,4,1,128]{4,3,2,1,0:T(1,128)S(1)}, f32[2,4,4,1,128]{4,3,2,1,0:T(1,128)S(1)}, u32[]{:S(2)}, u32[]{:S(2)}) collective-permute-start(f32[2,4,4,1,128]{4,3,2,1,0:T(1,128)S(1)} %get-tuple-element.125), channel_id=1, source_target_pairs={{1,0},{2,1},{3,2},{5,4},{6,5},{7,6},{9,8},{10,9},{11,10},{13,12},{... | collective-permute-start | bytes 49160 | tf_op jit(solution)/shard_map/ppermute | solution.py:24
  349.8 18.8 %collective-permute-start.23 = (f32[2,4,4,1,128]{4,3,2,1,0:T(1,128)S(1)}, f32[2,4,4,1,128]{4,3,2,1,0:T(1,128)S(1)}, u32[]{:S(2)}, u32[]{:S(2)}) collective-permute-start(f32[2,4,4,1,128]{4,3,2,1,0:T(1,128)S(1)} %get-tuple-element.126), channel_id=1, source_target_pairs={{0,1},{1,2},{2,3},{4,5},{5,6},{6,7},{8,9},{9,10},{10,11},{12,13},{... | collective-permute-start | bytes 49160 | tf_op jit(solution)/shard_map/ppermute | solution.py:23
  354.6 14.0 %collective-permute-start.20 = (f32[2,4,4,32,1]{4,3,2,1,0:T(8,128)S(1)}, f32[2,4,4,32,1]{4,3,2,1,0:T(8,128)S(1)}, u32[]{:S(2)}, u32[]{:S(2)}) collective-permute-start(f32[2,4,4,32,1]{4,3,2,1,0:T(8,128)S(1)} %get-tuple-element.123), channel_id=1, source_target_pairs={{4,0},{8,4},{12,8},{16,12},{20,16},{24,20},{28,24},{0,28},{5,1},{9... | collective-permute-start | bytes 12296 | tf_op jit(solution)/shard_map/ppermute | solution.py:24
  358.1 10.6 %collective-permute-start.21 = (f32[2,4,4,32,1]{4,3,2,1,0:T(8,128)S(1)}, f32[2,4,4,32,1]{4,3,2,1,0:T(8,128)S(1)}, u32[]{:S(2)}, u32[]{:S(2)}) collective-permute-start(f32[2,4,4,32,1]{4,3,2,1,0:T(8,128)S(1)} %get-tuple-element.124), channel_id=1, source_target_pairs={{0,4},{4,8},{8,12},{12,16},{16,20},{20,24},{24,28},{28,0},{1,5},{5... | collective-permute-start | bytes 12296 | tf_op jit(solution)/shard_map/ppermute | solution.py:23
where the time goes:
time: 372 us; the launch traced here: 370 us
  waiting for transfers between devices  99.4 us (27%)
  matrix products  94.6 us (25%)
  local copies, waits for them, and re-layouts  82.7 us (22%)
  starting transfers between devices  68.5 us (18%)
  other arithmetic  23.7 us (6%)
    dot_general x7, matrix products, build_tiles(): return jnp.einsum('dcaj,dajp->dacp', innov_f32, weight, precision=HIGHEST)  83.4 us
    ppermute x12, waiting for transfers between devices, with_halo(): after = lax.ppermute(leading, axis, down)  47 us
    ppermute x12, starting transfers between devices, with_halo(): before = lax.ppermute(last, axis, up)  29.7 us
    reshape x2, local copies, waits for them, and re-layouts, place_tiles(): summed.reshape(slot_total, VARS, LEV, block_rows, block_cols, TILE, TILE)  25.8 us
    all_to_all x1, waiting for transfers between devices, shards(): lax.all_to_all(innovations, ('lon', 'lat'), split_axis=1, concat_axis=1,...  23.7 us
    ppermute x12, starting transfers between devices, with_halo(): after = lax.ppermute(leading, axis, down)  21.1 us
    squeeze x6, local copies, waits for them, and re-layouts, shards(): forcing[later]  19 us
    dynamic_update_slice x7, local copies, waits for them, and re-layouts, shards(): lax.map(build_slot, (got_values, got_fractions, got_cells, got_counts))  11.3 us
  transfers between devices with their start and end apart: 29, of which 14 were waited for; matrix products, arithmetic and copies ran while one was open for 9% of the time, Pallas kernels for 0%

commit v1 on v0

v1 whole, which is shorter than its diff:
```python
import functools

import jax
import jax.numpy as jnp
from jax import lax
from jax.experimental import pallas as pl
from jax.experimental.pallas import tpu as pltpu
from jax.sharding import PartitionSpec as P

VARS = 4
LEV = 4
CH = 16
TILE = 16
KAPPA = 0.125
EDGE = 8
GROUP = 4
MESH = pl.DeviceIdType.MESH


def kernel(
    n_lon, n_lat, slots, lat_cells, lon_cells,
    mix_ref, innov_ref, meta_ref, u_ref, v_ref, out_ref,
    got_innov, got_meta, rows_buf, acc, field, mixed, wind, wind_send, wind_got, lon_send, lon_got,
    own_sem, innov_send, innov_recv, meta_send, meta_recv,
    wlat_send, wlat_recv, wlon_send, wlon_recv, flat_send, flat_recv, flon_send, flon_recv,
):
    devices = n_lon * n_lat
    my_lon, my_lat = lax.axis_index("lon"), lax.axis_index("lat")
    me = my_lon * n_lat + my_lat
    width = got_innov.shape[-1]
    span = GROUP * width
    tall = lat_cells + 2 * EDGE
    low, high = EDGE, EDGE + lat_cells

    lat_up = (my_lon, (my_lat + 1) % n_lat)
    lat_down = (my_lon, (my_lat + n_lat - 1) % n_lat)
    lon_up = ((my_lon + 1) % n_lon, my_lat)
    lon_down = ((my_lon + n_lon - 1) % n_lon, my_lat)

    barrier = pltpu.get_barrier_semaphore()

    @pl.loop(1, devices)
    def _(k):
        to = (me + k) % devices
        pl.semaphore_signal(barrier, inc=1, device_id=(to // n_lat, to % n_lat), device_id_type=MESH)

    own_a = pltpu.make_async_copy(innov_ref.at[:, me], got_innov.at[0], own_sem.at[0])
    own_b = pltpu.make_async_copy(meta_ref.at[me], got_meta.at[0], own_sem.at[1])
    own_a.start()
    own_b.start()
    wind[0:LEV, low:high, 0:lon_cells] = u_ref[...]
    wind[LEV : 2 * LEV, low:high, 0:lon_cells] = v_ref[...]
    pl.semaphore_wait(barrier, devices - 1)

    def lat_pair(buffer, send, recv):
        down = pltpu.make_async_remote_copy(
            src_ref=buffer.at[:, low : low + EDGE, 0:lon_cells],
            dst_ref=buffer.at[:, high : high + EDGE, 0:lon_cells],
            send_sem=send.at[0], recv_sem=recv.at[0], device_id=lat_down, device_id_type=MESH,
        )
        up = pltpu.make_async_remote_copy(
            src_ref=buffer.at[:, high - EDGE : high, 0:lon_cells],
            dst_ref=buffer.at[:, 0:low, 0:lon_cells],
            send_sem=send.at[1], recv_sem=recv.at[1], device_id=lat_up, device_id_type=MESH,
        )
        return down, up

    def lon_pair(send_buf, got_buf, send, recv):
        down = pltpu.make_async_remote_copy(
            src_ref=send_buf.at[0], dst_ref=got_buf.at[0],
            send_sem=send.at[0], recv_sem=recv.at[0], device_id=lon_down, device_id_type=MESH,
        )
        up = pltpu.make_async_remote_copy(
            src_ref=send_buf.at[1], dst_ref=got_buf.at[1],
            send_sem=send.at[1], recv_sem=recv.at[1], device_id=lon_up, device_id_type=MESH,
        )
        return down, up

    lane = lax.broadcasted_iota(jnp.int32, (tall, lon_cells), 1)

    def pack(source, count, target):
        first = jnp.zeros((tall, lon_cells), jnp.float32)
        last = first
        for c in range(count):
            body = source[c, :, 0:lon_cells]
            here = (lane >= EDGE * c) & (lane < EDGE * (c + 1))
            a = body if c == 0 else pltpu.roll(body, EDGE * c, 1)
            shift = (EDGE * (c + 1)) % lon_cells
            b = body if shift == 0 else pltpu.roll(body, shift, 1)
            first = jnp.where(here, a, first)
            last = jnp.where(here, b, last)
        target[0] = first
        target[1] = last

    def unpack(got, count, target):
        after, before = got[0], got[1]
        for c in range(count):
            back = (lon_cells - EDGE * c) % lon_cells
            a = after if back == 0 else pltpu.roll(after, back, 1)
            shift = (lon_cells - EDGE - EDGE * c) % lon_cells
            b = before if shift == 0 else pltpu.roll(before, shift, 1)
            target[c, :, lon_cells : 2 * lon_cells] = jnp.where(lane < EDGE, a, b)

    wind_lat = lat_pair(wind, wlat_send, wlat_recv)
    for copy in wind_lat:
        copy.start()

    def exchange(k):
        to = (me + k) % devices
        where = (to // n_lat, to % n_lat)
        big = pltpu.make_async_remote_copy(
            src_ref=innov_ref.at[:, to], dst_ref=got_innov.at[k],
            send_sem=innov_send.at[k], recv_sem=innov_recv.at[k], device_id=where, device_id_type=MESH,
        )
        small = pltpu.make_async_remote_copy(
            src_ref=meta_ref.at[to], dst_ref=got_meta.at[k],
            send_sem=meta_send.at[k], recv_sem=meta_recv.at[k], device_id=where, device_id_type=MESH,
        )
        return small, big

    @pl.loop(1, devices)
    def _(k):
        for copy in exchange(k):
            copy.start()

    @pl.loop(0, slots)
    def _(s):
        acc[s] = jnp.zeros(acc.shape[1:], jnp.float32)

    own_a.wait()
    own_b.wait()
    for copy in wind_lat:
        copy.wait()
    pack(wind, 2 * LEV, wind_send)
    wind_lon = lon_pair(wind_send, wind_got, wlon_send, wlon_recv)
    for copy in wind_lon:
        copy.start()

    row_id = lax.broadcasted_iota(jnp.int32, (lat_cells, span), 0).astype(jnp.float32)
    col_id = lax.broadcasted_iota(jnp.int32, (lon_cells, span), 0).astype(jnp.float32)
    contract = (((1,), (1,)), ((), ()))

    @pl.loop(0, devices // GROUP)
    def _(g):
        for i in range(GROUP):
            k = g * GROUP + i

            @pl.when(k > 0)
            def _():
                for copy in exchange(k):
                    copy.wait_recv()

            numbers = got_meta[k].astype(jnp.float32)
            for s in range(slots):
                rows_buf[s, 0:4, i * width : (i + 1) * width] = numbers[4 * s : 4 * s + 4]

        @pl.loop(0, slots)
        def _(s):
            values = jnp.concatenate(
                [got_innov[g * GROUP + i, s] for i in range(GROUP)], axis=1
            ).astype(jnp.float32)
            frac_y, frac_x = rows_buf[s, 0:1], rows_buf[s, 1:2]
            row, col = rows_buf[s, 2:3], rows_buf[s, 3:4]
            at_row = jnp.where(row_id == row, 1.0, 0.0).astype(jnp.bfloat16)
            at_next = jnp.where(row_id == row + 1.0, 1.0, 0.0).astype(jnp.bfloat16)
            hit = col_id == col
            cols = jnp.concatenate(
                [jnp.where(hit, 1.0, 0.0).astype(jnp.bfloat16), jnp.where(hit, frac_x, 0.0).astype(jnp.bfloat16)], axis=0
            )
            lower = values * (1.0 - frac_y)
            upper = values * frac_y
            lower_hi = lower.astype(jnp.bfloat16).astype(jnp.float32)
            upper_hi = upper.astype(jnp.bfloat16).astype(jnp.float32)
            lower_lo = lower - lower_hi
            upper_lo = upper - upper_hi

            def spread(low_part, up_part):
                pieces = []
                for c in range(CH):
                    a = jnp.broadcast_to(low_part[c : c + 1], (16, span)).astype(jnp.bfloat16)
                    b = jnp.broadcast_to(up_part[c : c + 1], (16, span)).astype(jnp.bfloat16)
                    for r in range(0, lat_cells, 16):
                        pieces.append(a * at_row[r : r + 16] + b * at_next[r : r + 16])
                return jnp.concatenate(pieces, axis=0)

            total = lax.dot_general(
                spread(lower_hi, upper_hi), cols, contract, preferred_element_type=jnp.float32
            )
            total = total + lax.dot_general(
                spread(lower_lo, upper_lo), cols, contract, preferred_element_type=jnp.float32
            )
            acc[s] += total

    def settle(s):
        plain = acc[s, :, 0:lon_cells]
        part = acc[s, :, lon_cells : 2 * lon_cells]
        whole = plain - part + pltpu.roll(part, 1, 1)
        field[s, :, low:high, 0:lon_cells] = whole.reshape(CH, lat_cells, lon_cells)

    lat_copies = {}
    for s in range(slots - 1, -1, -1):
        settle(s)
        if s > 0:
            lat_copies[s] = lat_pair(field.at[s], flat_send.at[s], flat_recv.at[s])
            for copy in lat_copies[s]:
                copy.start()
    for copy in wind_lon:
        copy.wait()
    unpack(wind_got, 2 * LEV, wind)
    lon_copies = {}
    for s in range(slots - 1, 0, -1):
        for copy in lat_copies[s]:
            copy.wait()
        pack(field.at[s], CH, lon_send.at[s])
        lon_copies[s] = lon_pair(lon_send.at[s], lon_got.at[s], flon_send.at[s], flon_recv.at[s])
        for copy in lon_copies[s]:
            copy.start()

    row_at = lax.broadcasted_iota(jnp.int32, (tall, 2 * lon_cells), 0)
    first = jnp.where(my_lat == 0, low, 0)
    last = jnp.where(my_lat == n_lat - 1, high, tall)
    inside = (row_at >= first) & (row_at < last)

    for s in range(slots - 1, -1, -1):
        if s > 0:
            for copy in lon_copies[s]:
                copy.wait()
            unpack(lon_got.at[s], CH, field.at[s])
        if s == slots - 1:
            continue
        older = s + 1

        @pl.loop(0, CH)
        def _(c):
            total = mix_ref[0, c] * field[older, 0]
            for d in range(1, CH):
                total = total + mix_ref[d, c] * field[older, d]
            total = jnp.where(inside, total, 0.0)
            level = c % LEV
            eastward = (0.5 * wind[level]) * total
            northward = (0.5 * wind[LEV + level]) * total
            near = KAPPA * total
            result = (
                (1.0 - 4.0 * KAPPA) * total
                + pltpu.roll(near + eastward, 2 * lon_cells - 1, 1)
                + pltpu.roll(near - eastward, 1, 1)
                + pltpu.roll(near + northward, tall - 1, 0)
                + pltpu.roll(near - northward, 1, 0)
            )
            if s > 0:
                mixed[c] = result
            else:
                out_ref[c] = result[low:high, 0:lon_cells] + field[0, c, low:high, 0:lon_cells]

        if s > 0:

            @pl.loop(0, CH)
            def _(c):
                field[s, c] += mixed[c]

    @pl.loop(1, devices)
    def _(k):
        for copy in exchange(k):
            copy.wait_send()


def shards(n_lon, n_lat, innovations, fractions, cell_index, counts, blocks, u_wind, v_wind, channel_mix):
    slots, devices, channels, width = innovations.shape
    lat_cells, lon_cells = u_wind.shape[1:]
    across = lon_cells // TILE
    tiles = counts.shape[2]
    per_tile = width // tiles
    within = lax.broadcasted_iota(jnp.int32, (1, 1, tiles, per_tile), 3)
    live = within < counts[..., None]
    cell = cell_index.reshape(slots, devices, tiles, per_tile)
    block = blocks[..., None]
    row = jnp.where(live, (block // across) * TILE + cell // TILE, -100)
    col = (block % across) * TILE + cell % TILE
    places = jnp.stack([row, col], axis=2).reshape(slots, devices, 2, width).astype(jnp.bfloat16)
    meta = jnp.concatenate([fractions, places], axis=2)
    meta = jnp.transpose(meta, (1, 0, 2, 3)).reshape(devices, 4 * slots, width)
    meta_rows = -(-4 * slots // 16) * 16
    meta = jnp.pad(meta, ((0, 0), (0, meta_rows - 4 * slots), (0, 0)))

    tall, wide = lat_cells + 2 * EDGE, 2 * lon_cells
    f32, bf16, dma = jnp.float32, jnp.bfloat16, pltpu.SemaphoreType.DMA
    vmem = pl.BlockSpec(memory_space=pltpu.VMEM)
    out = pl.pallas_call(
        functools.partial(kernel, n_lon, n_lat, slots, lat_cells, lon_cells),
        out_shape=jax.ShapeDtypeStruct((CH, lat_cells, lon_cells), f32),
        in_specs=[
            pl.BlockSpec(memory_space=pltpu.SMEM),
            pl.BlockSpec(memory_space=pl.ANY),
            pl.BlockSpec(memory_space=pl.ANY),
            vmem,
            vmem,
        ],
        out_specs=vmem,
        scratch_shapes=[
            pltpu.VMEM((devices, slots, channels, width), bf16),
            pltpu.VMEM((devices, meta_rows, width), bf16),
            pltpu.VMEM((slots, 8, GROUP * width), f32),
            pltpu.VMEM((slots, CH * lat_cells, wide), f32),
            pltpu.VMEM((slots, CH, tall, wide), f32),
            pltpu.VMEM((CH, tall, wide), f32),
            pltpu.VMEM((2 * LEV, tall, wide), f32),
            pltpu.VMEM((2, tall, lon_cells), f32),
            pltpu.VMEM((2, tall, lon_cells), f32),
            pltpu.VMEM((slots, 2, tall, lon_cells), f32),
            pltpu.VMEM((slots, 2, tall, lon_cells), f32),
            dma((2,)),
            dma((devices,)),
            dma((devices,)),
            dma((devices,)),
            dma((devices,)),
            dma((2,)),
            dma((2,)),
            dma((2,)),
            dma((2,)),
            dma((slots, 2)),
            dma((slots, 2)),
            dma((slots, 2)),
            dma((slots, 2)),
        ],
        compiler_params=pltpu.CompilerParams(
            collective_id=0, has_side_effects=True, vmem_limit_bytes=48 * 1024 * 1024
        ),
    )(channel_mix, innovations, meta, u_wind, v_wind)
    return out.reshape(VARS, LEV, lat_cells, lon_cells)


def solution(mesh):
    in_specs = (
        P(None, ("lon", "lat"), None, None),
        P(None, ("lon", "lat"), None, None),
        P(None, ("lon", "lat"), None),
        P(None, ("lon", "lat"), None),
        P(None, ("lon", "lat"), None),
        P(None, "lat", "lon"),
        P(None, "lat", "lon"),
        P(),
    )
    out_specs = P(None, None, "lat", "lon")
    body = functools.partial(shards, mesh.shape["lon"], mesh.shape["lat"])
    return jax.shard_map(body, mesh=mesh, in_specs=in_specs, out_specs=out_specs, check_vma=False)
```

time: 372 us -> 92.9 us (0.25)
  the two profiles are of different devices: /device:TPU:0 before, /device:TPU:28 now
where the time goes in v1:
time: 92.9 us; the launch traced here: 92.7 us
  Pallas kernels  86.2 us (93%)
  local copies, waits for them, and re-layouts  5.18 us (6%)
  other arithmetic  1.19 us (1%)
    pallas_call x1, Pallas kernels, shards(): pl.pallas_call(functools.partial(kernel, n_lon, n_lat, slots, lat_cells,...  86.2 us
    unnamed x17, local copies, waits for them, and re-layouts  3.74 us

profile of v1, /device:TPU:28, one launch (start us, length us, event | category | flops | bytes accessed | tf_op | source)
XLA Modules:
  0.0 92.7 jit_solution(588261403992496480)
XLA Ops:
  0.0 0.7 fusion.10
  0.7 0.1 copy.16
  0.9 0.3 add.52
  1.2 0.2 add.53
  1.3 0.1 copy.17
  1.4 0.3 add.56
  1.8 0.0 copy-start.6
  1.8 0.2 add.57
  1.9 0.5 copy-done.6
  2.5 0.1 copy.15
  2.6 0.3 iota_compare_fusion
  2.9 0.0 copy-start.5
  2.9 0.1 lt.28
  3.0 0.8 copy-done.5
  3.8 0.0 copy-start.4
  3.8 0.1 fusion.8
  3.9 0.0 copy-start
  3.9 0.7 copy-done.4
  4.7 0.1 copy.21
  4.8 0.0 copy-start.1
  4.9 0.0 copy-start.2
  4.9 0.0 copy-start.3
  4.9 0.2 copy-done
  5.1 0.6 copy-done.1
  5.8 0.0 copy-done.2
  5.8 0.0 copy-done.3
  5.8 86.2 %shard_map.82 = f32[16,32,128]{2,1,0:T(8,128)S(1)} custom-call(f32[16,16]{1,0:T(8,128)S(1)} %copy-done.3, bf16[7,32,16,128]{3,2,1,0:T(8,128)(2,1)S(1)} %copy-done, bf16[32,32,128]{2,1,0:T(8,128)(2,1)S(1)} %pad.4.meta_ref, f32[4,32,128]{2,1,0:T(8,128)S(1)} %copy-done.1, f32[4,32,128]{2,1,0:T(8,128)S(1)} %copy-done.2), custom_call_target="tpu_custom_call" | custom-call | tf_op jit(solution)/shard_map/pallas_call | solution.py:288
  91.9 0.7 copy.23
  (3 shorter events, 0.1 us)
Async XLA Ops:
  1.8 0.7 copy-start.6
  2.9 0.9 copy-start.5
  3.8 0.9 copy-start.4
  3.9 1.2 %copy-start = (bf16[7,32,16,128]{3,2,1,0:T(8,128)(2,1)S(1)}, bf16[7,32,16,128]{3,2,1,0:T(8,128)(2,1)}, u32[]{:S(2)}) copy-start(bf16[7,32,16,128]{3,2,1,0:T(8,128)(2,1)} %innov_ref.1) | copy-start | bytes 2752516
  4.8 0.9 copy-start.1
  4.9 0.9 copy-start.2
  4.9 0.9 copy-start.3

commit v2 on v1

--- a/solution.py
+++ b/solution.py
@@ -14,13 +14,14 @@
 KAPPA = 0.125
 EDGE = 8
 GROUP = 4
+AHEAD = 2
 MESH = pl.DeviceIdType.MESH
 
 
 def kernel(
     n_lon, n_lat, slots, lat_cells, lon_cells,
     mix_ref, innov_ref, meta_ref, u_ref, v_ref, out_ref,
-    got_innov, got_meta, rows_buf, acc, field, mixed, wind, wind_send, wind_got, lon_send, lon_got,
+    got_innov, got_meta, rows_buf, acc, field, wind, wind_send, wind_got, lon_send, lon_got,
     own_sem, innov_send, innov_recv, meta_send, meta_recv,
     wlat_send, wlat_recv, wlon_send, wlon_recv, flat_send, flat_recv, flon_send, flon_recv,
 ):
@@ -31,6 +32,7 @@
     span = GROUP * width
     tall = lat_cells + 2 * EDGE
     low, high = EDGE, EDGE + lat_cells
+    metas = got_meta.shape[0]
 
     lat_up = (my_lon, (my_lat + 1) % n_lat)
     lat_down = (my_lon, (my_lat + n_lat - 1) % n_lat)
@@ -44,8 +46,8 @@
         to = (me + k) % devices
         pl.semaphore_signal(barrier, inc=1, device_id=(to // n_lat, to % n_lat), device_id_type=MESH)
 
-    own_a = pltpu.make_async_copy(innov_ref.at[:, me], got_innov.at[0], own_sem.at[0])
-    own_b = pltpu.make_async_copy(meta_ref.at[me], got_meta.at[0], own_sem.at[1])
+    own_a = pltpu.make_async_copy(innov_ref.at[:, me], got_innov.at[:, 0], own_sem.at[0])
+    own_b = pltpu.make_async_copy(meta_ref.at[:, me], got_meta.at[:, 0], own_sem.at[1])
     own_a.start()
     own_b.start()
     wind[0:LEV, low:high, 0:lon_cells] = u_ref[...]
@@ -101,66 +103,106 @@
             b = before if shift == 0 else pltpu.roll(before, shift, 1)
             target[c, :, lon_cells : 2 * lon_cells] = jnp.where(lane < EDGE, a, b)
 
+    def field_lat(s):
+        return lat_pair(field.at[s], flat_send.at[s], flat_recv.at[s])
+
+    def field_lon(s):
+        return lon_pair(lon_send.at[s], lon_got.at[s], flon_send.at[s], flon_recv.at[s])
+
+    def send_slot(s):
+        @pl.loop(1, devices)
+        def _(k):
+            to = (me + k) % devices
+            pltpu.make_async_remote_copy(
+                src_ref=innov_ref.at[s, to], dst_ref=got_innov.at[s, k],
+                send_sem=innov_send.at[s], recv_sem=innov_recv.at[s],
+                device_id=(to // n_lat, to % n_lat), device_id_type=MESH,
+            ).start()
+
+    def slot_total(s):
+        return pltpu.make_async_remote_copy(
+            src_ref=got_innov.at[s, 1:devices], dst_ref=got_innov.at[s, 1:devices],
+            send_sem=innov_send.at[s], recv_sem=innov_recv.at[s], device_id=lat_up, device_id_type=MESH,
+        )
+
+    def send_meta(m):
+        @pl.loop(1, devices)
+        def _(k):
+            to = (me + k) % devices
+            pltpu.make_async_remote_copy(
+                src_ref=meta_ref.at[m, to], dst_ref=got_meta.at[m, k],
+                send_sem=meta_send.at[m], recv_sem=meta_recv.at[m],
+                device_id=(to // n_lat, to % n_lat), device_id_type=MESH,
+            ).start()
+
+    def meta_total(m):
+        return pltpu.make_async_remote_copy(
+            src_ref=got_meta.at[m, 1:devices], dst_ref=got_meta.at[m, 1:devices],
+            send_sem=meta_send.at[m], recv_sem=meta_recv.at[m], device_id=lat_up, device_id_type=MESH,
+        )
+
     wind_lat = lat_pair(wind, wlat_send, wlat_recv)
+    wind_lon = lon_pair(wind_send, wind_got, wlon_send, wlon_recv)
     for copy in wind_lat:
         copy.start()
-
-    def exchange(k):
-        to = (me + k) % devices
-        where = (to // n_lat, to % n_lat)
-        big = pltpu.make_async_remote_copy(
-            src_ref=innov_ref.at[:, to], dst_ref=got_innov.at[k],
-            send_sem=innov_send.at[k], recv_sem=innov_recv.at[k], device_id=where, device_id_type=MESH,
-        )
-        small = pltpu.make_async_remote_copy(
-            src_ref=meta_ref.at[to], dst_ref=got_meta.at[k],
-            send_sem=meta_send.at[k], recv_sem=meta_recv.at[k], device_id=where, device_id_type=MESH,
-        )
-        return small, big
-
-    @pl.loop(1, devices)
-    def _(k):
-        for copy in exchange(k):
-            copy.start()
-
-    @pl.loop(0, slots)
-    def _(s):
-        acc[s] = jnp.zeros(acc.shape[1:], jnp.float32)
-
+    send_meta(0)
+    for n in range(AHEAD):
+        send_slot(slots - 1 - n)
     own_a.wait()
     own_b.wait()
     for copy in wind_lat:
         copy.wait()
     pack(wind, 2 * LEV, wind_send)
-    wind_lon = lon_pair(wind_send, wind_got, wlon_send, wlon_recv)
     for copy in wind_lon:
         copy.start()
 
     row_id = lax.broadcasted_iota(jnp.int32, (lat_cells, span), 0).astype(jnp.float32)
     col_id = lax.broadcasted_iota(jnp.int32, (lon_cells, span), 0).astype(jnp.float32)
     contract = (((1,), (1,)), ((), ()))
-
-    @pl.loop(0, devices // GROUP)
-    def _(g):
-        for i in range(GROUP):
-            k = g * GROUP + i
-
-            @pl.when(k > 0)
-            def _():
-                for copy in exchange(k):
-                    copy.wait_recv()
-
-            numbers = got_meta[k].astype(jnp.float32)
-            for s in range(slots):
-                rows_buf[s, 0:4, i * width : (i + 1) * width] = numbers[4 * s : 4 * s + 4]
-
-        @pl.loop(0, slots)
-        def _(s):
+    row_at = lax.broadcasted_iota(jnp.int32, (tall, 2 * lon_cells), 0)
+    first_row = jnp.where(my_lat == 0, low, 0)
+    last_row = jnp.where(my_lat == n_lat - 1, high, tall)
+    inside = (row_at >= first_row) & (row_at < last_row)
+
+    def stepped(older, c):
+        total = mix_ref[0, c] * field[older, 0]
+        for d in range(1, CH):
+            total = total + mix_ref[d, c] * field[older, d]
+        total = jnp.where(inside, total, 0.0)
+        level = c % LEV
+        eastward = (0.5 * wind[level]) * total
+        northward = (0.5 * wind[LEV + level]) * total
+        near = KAPPA * total
+        return (
+            (1.0 - 4.0 * KAPPA) * total
+            + pltpu.roll(near + eastward, 2 * lon_cells - 1, 1)
+            + pltpu.roll(near - eastward, 1, 1)
+            + pltpu.roll(near + northward, tall - 1, 0)
+            + pltpu.roll(near - northward, 1, 0)
+        )
+
+    def take_meta(m):
+        meta_total(m).wait_recv()
+
+        @pl.loop(0, devices // GROUP)
+        def _(g):
+            for i in range(GROUP):
+                numbers = got_meta[m, g * GROUP + i].astype(jnp.float32)
+                for j in range(4):
+                    s = slots - 1 - (4 * m + j)
+                    if s >= 0:
+                        rows_buf[s, g, 0:4, i * width : (i + 1) * width] = numbers[4 * j : 4 * j + 4]
+
+    def gather_slot(s):
+        acc[...] = jnp.zeros(acc.shape, jnp.float32)
+
+        @pl.loop(0, devices // GROUP)
+        def _(g):
             values = jnp.concatenate(
-                [got_innov[g * GROUP + i, s] for i in range(GROUP)], axis=1
+                [got_innov[s, g * GROUP + i] for i in range(GROUP)], axis=1
             ).astype(jnp.float32)
-            frac_y, frac_x = rows_buf[s, 0:1], rows_buf[s, 1:2]
-            row, col = rows_buf[s, 2:3], rows_buf[s, 3:4]
+            frac_y, frac_x = rows_buf[s, g, 0:1], rows_buf[s, g, 1:2]
+            row, col = rows_buf[s, g, 2:3], rows_buf[s, g, 3:4]
             at_row = jnp.where(row_id == row, 1.0, 0.0).astype(jnp.bfloat16)
             at_next = jnp.where(row_id == row + 1.0, 1.0, 0.0).astype(jnp.bfloat16)
             hit = col_id == col
@@ -189,79 +231,83 @@
             total = total + lax.dot_general(
                 spread(lower_lo, upper_lo), cols, contract, preferred_element_type=jnp.float32
             )
-            acc[s] += total
-
-    def settle(s):
-        plain = acc[s, :, 0:lon_cells]
-        part = acc[s, :, lon_cells : 2 * lon_cells]
+            acc[...] += total
+
+        plain = acc[:, 0:lon_cells]
+        part = acc[:, lon_cells : 2 * lon_cells]
         whole = plain - part + pltpu.roll(part, 1, 1)
         field[s, :, low:high, 0:lon_cells] = whole.reshape(CH, lat_cells, lon_cells)
 
-    lat_copies = {}
-    for s in range(slots - 1, -1, -1):
-        settle(s)
-        if s > 0:
-            lat_copies[s] = lat_pair(field.at[s], flat_send.at[s], flat_recv.at[s])
-            for copy in lat_copies[s]:
+    @pl.loop(0, slots)
+    def _(n):
+        s = slots - 1 - n
+
+        @pl.when(n >= 1)
+        def _():
+            for copy in field_lat(s + 1):
+                copy.wait()
+            pack(field.at[s + 1], CH, lon_send.at[s + 1])
+            for copy in field_lon(s + 1):
                 copy.start()
-    for copy in wind_lon:
-        copy.wait()
-    unpack(wind_got, 2 * LEV, wind)
-    lon_copies = {}
-    for s in range(slots - 1, 0, -1):
-        for copy in lat_copies[s]:
-            copy.wait()
-        pack(field.at[s], CH, lon_send.at[s])
-        lon_copies[s] = lon_pair(lon_send.at[s], lon_got.at[s], flon_send.at[s], flon_recv.at[s])
-        for copy in lon_copies[s]:
-            copy.start()
-
-    row_at = lax.broadcasted_iota(jnp.int32, (tall, 2 * lon_cells), 0)
-    first = jnp.where(my_lat == 0, low, 0)
-    last = jnp.where(my_lat == n_lat - 1, high, tall)
-    inside = (row_at >= first) & (row_at < last)
-
-    for s in range(slots - 1, -1, -1):
-        if s > 0:
-            for copy in lon_copies[s]:
+
+        slot_total(s).wait_recv()
+
+        @pl.when(n + AHEAD < slots)
+        def _():
+            send_slot(s - AHEAD)
+
+        for m in range(1, metas):
+
+            @pl.when(n + AHEAD == 4 * m)
+            def _():
+                send_meta(m)
+
+        for m in range(metas):
+
+            @pl.when(n == 4 * m)
+            def _():
+                take_meta(m)
+
+        gather_slot(s)
+
+        @pl.when(n < slots - 1)
+        def _():
+            for copy in field_lat(s):
+                copy.start()
+
+        @pl.when(n == 1)
+        def _():
+            for copy in wind_lon:
                 copy.wait()
-            unpack(lon_got.at[s], CH, field.at[s])
-        if s == slots - 1:
-            continue
-        older = s + 1
-
-        @pl.loop(0, CH)
-        def _(c):
-            total = mix_ref[0, c] * field[older, 0]
-            for d in range(1, CH):
-                total = total + mix_ref[d, c] * field[older, d]
-            total = jnp.where(inside, total, 0.0)
-            level = c % LEV
-            eastward = (0.5 * wind[level]) * total
-            northward = (0.5 * wind[LEV + level]) * total
-            near = KAPPA * total
-            result = (
-                (1.0 - 4.0 * KAPPA) * total
-                + pltpu.roll(near + eastward, 2 * lon_cells - 1, 1)
-                + pltpu.roll(near - eastward, 1, 1)
-                + pltpu.roll(near + northward, tall - 1, 0)
-                + pltpu.roll(near - northward, 1, 0)
-            )
-            if s > 0:
-                mixed[c] = result
-            else:
-                out_ref[c] = result[low:high, 0:lon_cells] + field[0, c, low:high, 0:lon_cells]
-
-        if s > 0:
-
+            unpack(wind_got, 2 * LEV, wind)
+
+        @pl.when(n >= 1)
+        def _():
+            for copy in field_lon(s + 1):
+                copy.wait_recv()
+            unpack(lon_got.at[s + 1], CH, field.at[s + 1])
+
+        @pl.when(n >= 2)
+        def _():
             @pl.loop(0, CH)
             def _(c):
-                field[s, c] += mixed[c]
-
-    @pl.loop(1, devices)
-    def _(k):
-        for copy in exchange(k):
-            copy.wait_send()
+                field[s + 1, c] += stepped(s + 2, c)
+
+    @pl.loop(0, CH)
+    def _(c):
+        out_ref[c] = stepped(1, c)[low:high, 0:lon_cells] + field[0, c, low:high, 0:lon_cells]
+
+    @pl.loop(0, slots)
+    def _(s):
+        slot_total(s).wait_send()
+
+        @pl.when(s > 0)
+        def _():
+            for copy in field_lon(s):
+                copy.wait_send()
+
+    for m in range(metas):
+        meta_total(m).wait_send()
 
 
 def shards(n_lon, n_lat, innovations, fractions, cell_index, counts, blocks, u_wind, v_wind, channel_mix):
@@ -278,9 +324,10 @@
     col = (block % across) * TILE + cell % TILE
     places = jnp.stack([row, col], axis=2).reshape(slots, devices, 2, width).astype(jnp.bfloat16)
     meta = jnp.concatenate([fractions, places], axis=2)
-    meta = jnp.transpose(meta, (1, 0, 2, 3)).reshape(devices, 4 * slots, width)
-    meta_rows = -(-4 * slots // 16) * 16
-    meta = jnp.pad(meta, ((0, 0), (0, meta_rows - 4 * slots), (0, 0)))
+    metas = -(-slots // 4)
+    meta = jnp.pad(meta[::-1], ((0, 4 * metas - slots), (0, 0), (0, 0), (0, 0)))
+    meta = meta.reshape(metas, 4, devices, 4, width)
+    meta = jnp.transpose(meta, (0, 2, 1, 3, 4)).reshape(metas, devices, 16, width)
 
     tall, wide = lat_cells + 2 * EDGE, 2 * lon_cells
     f32, bf16, dma = jnp.float32, jnp.bfloat16, pltpu.SemaphoreType.DMA
@@ -297,22 +344,21 @@
         ],
         out_specs=vmem,
         scratch_shapes=[
-            pltpu.VMEM((devices, slots, channels, width), bf16),
-            pltpu.VMEM((devices, meta_rows, width), bf16),
-            pltpu.VMEM((slots, 8, GROUP * width), f32),
-            pltpu.VMEM((slots, CH * lat_cells, wide), f32),
+            pltpu.VMEM((slots, devices, channels, width), bf16),
+            pltpu.VMEM((metas, devices, 16, width), bf16),
+            pltpu.VMEM((slots, devices // GROUP, 8, GROUP * width), f32),
+            pltpu.VMEM((CH * lat_cells, wide), f32),
             pltpu.VMEM((slots, CH, tall, wide), f32),
-            pltpu.VMEM((CH, tall, wide), f32),
             pltpu.VMEM((2 * LEV, tall, wide), f32),
             pltpu.VMEM((2, tall, lon_cells), f32),
             pltpu.VMEM((2, tall, lon_cells), f32),
             pltpu.VMEM((slots, 2, tall, lon_cells), f32),
             pltpu.VMEM((slots, 2, tall, lon_cells), f32),
             dma((2,)),
-            dma((devices,)),
-            dma((devices,)),
-            dma((devices,)),
-            dma((devices,)),
+            dma((slots,)),
+            dma((slots,)),
+            dma((metas,)),
+            dma((metas,)),
             dma((2,)),
             dma((2,)),
             dma((2,)),

time: 92.9 us -> 89.9 us (0.968)
  the two profiles are of different devices: /device:TPU:28 before, /device:TPU:0 now
where the time goes in v2:
time: 89.9 us; the launch traced here: 89.7 us
  Pallas kernels  82.5 us (92%)
  local copies, waits for them, and re-layouts  5.47 us (6%)
  other arithmetic  1.55 us (2%)
    pallas_call x1, Pallas kernels, shards(): pl.pallas_call(functools.partial(kernel, n_lon, n_lat, slots, lat_cells,...  82.5 us
    unnamed x16, local copies, waits for them, and re-layouts  3.71 us

profile of v2, /device:TPU:0, one launch (start us, length us, event | category | flops | bytes accessed | tf_op | source)
XLA Modules:
  0.0 89.7 jit_solution(1839935458262930573)
XLA Ops:
  0.0 0.7 fusion.10
  0.7 0.1 copy.16
  0.9 0.3 add.52
  1.2 0.2 add.53
  1.3 0.1 copy.17
  1.4 0.3 add.56
  1.8 0.0 copy-start.6
  1.8 0.2 add.57
  1.9 0.5 copy-done.6
  2.5 0.1 copy.15
  2.6 0.3 iota_compare_fusion
  2.9 0.0 copy-start.4
  2.9 0.1 lt.28
  3.0 0.8 copy-done.4
  3.8 0.1 fusion.8
  3.9 0.1 copy.18
  4.0 0.0 copy-start.5
  4.0 0.1 copy.19
  4.1 0.8 copy-done.5
  4.9 0.0 copy-start
  4.9 0.4 pad_maximum_fusion
  5.3 0.1 rev.3
  5.4 0.1 pad.4
  5.5 0.0 copy-start.1
  5.5 0.0 copy-start.2
  5.5 0.0 copy-start.3
  5.5 0.1 copy.20
  5.6 0.5 copy-done
  6.1 0.3 copy-done.1
  6.4 0.0 copy-done.2
  6.4 0.0 copy-done.3
  6.4 82.5 %shard_map.82 = f32[16,32,128]{2,1,0:T(8,128)S(1)} custom-call(f32[16,16]{1,0:T(8,128)S(1)} %copy-done.3, bf16[7,32,16,128]{3,2,1,0:T(8,128)(2,1)S(1)} %copy-done, bf16[2,32,16,128]{3,2,1,0:T(8,128)(2,1)S(1)} %bitcast.9, f32[4,32,128]{2,1,0:T(8,128)S(1)} %copy-done.1, f32[4,32,128]{2,1,0:T(8,128)S(1)} %copy-done.2), custom_call_target="tpu_custom_call" | custom-call | tf_op jit(solution)/shard_map/pallas_call | solution.py:335
  89.0 0.7 copy.22
Async XLA Ops:
  1.8 0.7 copy-start.6
  2.9 0.9 %copy-start.4 = (s32[7,32,128]{2,1,0:T(8,128)S(1)}, s32[7,32,128]{2,1,0:T(8,128)}, u32[]{:S(2)}) copy-start(s32[7,32,128]{2,1,0:T(8,128)} %param.10) | copy-start | bytes 344068
  4.0 0.9 %copy-start.5 = (bf16[7,32,2,128]{3,2,1,0:T(2,128)(2,1)S(1)}, bf16[7,32,2,128]{3,2,1,0:T(2,128)(2,1)}, u32[]{:S(2)}) copy-start(bf16[7,32,2,128]{3,2,1,0:T(2,128)(2,1)} %param.9) | copy-start | bytes 344068
  4.9 1.2 %copy-start = (bf16[7,32,16,128]{3,2,1,0:T(8,128)(2,1)S(1)}, bf16[7,32,16,128]{3,2,1,0:T(8,128)(2,1)}, u32[]{:S(2)}) copy-start(bf16[7,32,16,128]{3,2,1,0:T(8,128)(2,1)} %innov_ref.1) | copy-start | bytes 2752516
  5.5 0.9 %copy-start.1 = (f32[4,32,128]{2,1,0:T(8,128)S(1)}, f32[4,32,128]{2,1,0:T(8,128)}, u32[]{:S(2)}) copy-start(f32[4,32,128]{2,1,0:T(8,128)} %u_ref.1) | copy-start | bytes 196612
  5.5 0.9 %copy-start.2 = (f32[4,32,128]{2,1,0:T(8,128)S(1)}, f32[4,32,128]{2,1,0:T(8,128)}, u32[]{:S(2)}) copy-start(f32[4,32,128]{2,1,0:T(8,128)} %v_ref.1) | copy-start | bytes 196612
  5.5 0.9 %copy-start.3 = (f32[16,16]{1,0:T(8,128)S(1)}, f32[16,16]{1,0:T(8,128)}, u32[]{:S(2)}) copy-start(f32[16,16]{1,0:T(8,128)} %mix_ref.1) | copy-start | bytes 3076

commit v3 on v2

--- a/solution.py
+++ b/solution.py
@@ -156,8 +156,9 @@
     for copy in wind_lon:
         copy.start()
 
-    row_id = lax.broadcasted_iota(jnp.int32, (lat_cells, span), 0).astype(jnp.float32)
-    col_id = lax.broadcasted_iota(jnp.int32, (lon_cells, span), 0).astype(jnp.float32)
+    across = lon_cells // TILE
+    tile_id = lax.broadcasted_iota(jnp.int32, (TILE, span), 0).astype(jnp.float32)
+    lane_group = lax.broadcasted_iota(jnp.int32, (CH, lon_cells), 1) // TILE
     contract = (((1,), (1,)), ((), ()))
     row_at = lax.broadcasted_iota(jnp.int32, (tall, 2 * lon_cells), 0)
     first_row = jnp.where(my_lat == 0, low, 0)
@@ -200,43 +201,51 @@
         def _(g):
             values = jnp.concatenate(
                 [got_innov[s, g * GROUP + i] for i in range(GROUP)], axis=1
-            ).astype(jnp.float32)
+            )
             frac_y, frac_x = rows_buf[s, g, 0:1], rows_buf[s, g, 1:2]
-            row, col = rows_buf[s, g, 2:3], rows_buf[s, g, 3:4]
-            at_row = jnp.where(row_id == row, 1.0, 0.0).astype(jnp.bfloat16)
-            at_next = jnp.where(row_id == row + 1.0, 1.0, 0.0).astype(jnp.bfloat16)
-            hit = col_id == col
-            cols = jnp.concatenate(
-                [jnp.where(hit, 1.0, 0.0).astype(jnp.bfloat16), jnp.where(hit, frac_x, 0.0).astype(jnp.bfloat16)], axis=0
-            )
-            lower = values * (1.0 - frac_y)
-            upper = values * frac_y
-            lower_hi = lower.astype(jnp.bfloat16).astype(jnp.float32)
-            upper_hi = upper.astype(jnp.bfloat16).astype(jnp.float32)
-            lower_lo = lower - lower_hi
-            upper_lo = upper - upper_hi
-
-            def spread(low_part, up_part):
-                pieces = []
-                for c in range(CH):
-                    a = jnp.broadcast_to(low_part[c : c + 1], (16, span)).astype(jnp.bfloat16)
-                    b = jnp.broadcast_to(up_part[c : c + 1], (16, span)).astype(jnp.bfloat16)
-                    for r in range(0, lat_cells, 16):
-                        pieces.append(a * at_row[r : r + 16] + b * at_next[r : r + 16])
-                return jnp.concatenate(pieces, axis=0)
-
-            total = lax.dot_general(
-                spread(lower_hi, upper_hi), cols, contract, preferred_element_type=jnp.float32
-            )
-            total = total + lax.dot_general(
-                spread(lower_lo, upper_lo), cols, contract, preferred_element_type=jnp.float32
-            )
-            acc[...] += total
-
-        plain = acc[:, 0:lon_cells]
-        part = acc[:, lon_cells : 2 * lon_cells]
-        whole = plain - part + pltpu.roll(part, 1, 1)
-        field[s, :, low:high, 0:lon_cells] = whole.reshape(CH, lat_cells, lon_cells)
+            cell, block = rows_buf[s, g, 2:3], rows_buf[s, g, 3:4]
+            row = jnp.floor(cell * (1.0 / TILE))
+            col = cell - TILE * row
+            in_rows = jnp.where(tile_id == row, 1.0 - frac_y, jnp.where(tile_id == row + 1.0, frac_y, 0.0))
+            in_cols = jnp.where(tile_id == col, 1.0 - frac_x, jnp.where(tile_id == col + 1.0, frac_x, 0.0))
+            heads, tails = [], []
+            for r in range(TILE):
+                weight = in_rows[r : r + 1] * in_cols
+                head = weight.astype(jnp.bfloat16)
+                heads.append(head)
+                tails.append((weight - head.astype(jnp.float32)).astype(jnp.bfloat16))
+            weights = jnp.concatenate(heads + tails, axis=0)
+            placed = []
+            for b in range(lat_cells // TILE * across):
+                here = jnp.broadcast_to(jnp.where(block == float(b), 1.0, 0.0), (CH, span)).astype(jnp.bfloat16)
+                placed.append(values * here)
+            placed = jnp.concatenate(placed, axis=0)
+            both = lax.dot_general(weights, placed, contract, preferred_element_type=jnp.float32)
+            acc[...] += both[: TILE * TILE] + both[TILE * TILE :]
+
+        tiles = jnp.transpose(acc[...])
+        strips = []
+        for down in range(lat_cells // TILE):
+            for half in range(TILE // across):
+                x = []
+                for i in range(across):
+                    b = down * across + i
+                    x.append(tiles[b * CH : (b + 1) * CH, half * lon_cells : (half + 1) * lon_cells])
+                apart = 1
+                while apart < across:
+                    moved = list(x)
+                    for i in range(across):
+                        if i & apart == 0:
+                            j = i + apart
+                            moved[i] = jnp.where(lane_group & apart == 0, x[i], pltpu.roll(x[j], TILE * apart, 1))
+                            moved[j] = jnp.where(
+                                lane_group & apart == 0, pltpu.roll(x[i], lon_cells - TILE * apart, 1), x[j]
+                            )
+                    x = moved
+                    apart *= 2
+                strips += x
+        whole = jnp.stack(strips, axis=0)
+        field[s, :, low:high, 0:lon_cells] = jnp.swapaxes(whole, 0, 1)
 
     @pl.loop(0, slots)
     def _(n):
@@ -313,16 +322,12 @@
 def shards(n_lon, n_lat, innovations, fractions, cell_index, counts, blocks, u_wind, v_wind, channel_mix):
     slots, devices, channels, width = innovations.shape
     lat_cells, lon_cells = u_wind.shape[1:]
-    across = lon_cells // TILE
     tiles = counts.shape[2]
     per_tile = width // tiles
     within = lax.broadcasted_iota(jnp.int32, (1, 1, tiles, per_tile), 3)
     live = within < counts[..., None]
-    cell = cell_index.reshape(slots, devices, tiles, per_tile)
-    block = blocks[..., None]
-    row = jnp.where(live, (block // across) * TILE + cell // TILE, -100)
-    col = (block % across) * TILE + cell % TILE
-    places = jnp.stack([row, col], axis=2).reshape(slots, devices, 2, width).astype(jnp.bfloat16)
+    block = jnp.where(live, blocks[..., None], -1).reshape(slots, devices, width)
+    places = jnp.stack([cell_index, block], axis=2).astype(jnp.bfloat16)
     meta = jnp.concatenate([fractions, places], axis=2)
     metas = -(-slots // 4)
     meta = jnp.pad(meta[::-1], ((0, 4 * metas - slots), (0, 0), (0, 0), (0, 0)))
@@ -347,7 +352,7 @@
             pltpu.VMEM((slots, devices, channels, width), bf16),
             pltpu.VMEM((metas, devices, 16, width), bf16),
             pltpu.VMEM((slots, devices // GROUP, 8, GROUP * width), f32),
-            pltpu.VMEM((CH * lat_cells, wide), f32),
+            pltpu.VMEM((TILE * TILE, CH * lat_cells * lon_cells // TILE**2), f32),
             pltpu.VMEM((slots, CH, tall, wide), f32),
             pltpu.VMEM((2 * LEV, tall, wide), f32),
             pltpu.VMEM((2, tall, lon_cells), f32),

time: 89.9 us -> 84.6 us (0.941)
  Pallas kernels: 82.5 us -> 77.7 us
  other arithmetic: 1.55 us -> 0.42 us
    pallas_call x1, Pallas kernels: 82.5 us -> 77.7 us  [shards(): pl.pallas_call(functools.partial(kernel, n_lon, n_lat, slots, lat_cells,...]
    add x5 -> x0, local copies, waits for them, and re-layouts: 1.03 us -> none  [the longest x3 0.56 us: shards(): col = block % across * TILE + cell % TILE]
    unnamed x16 -> x17, local copies, waits for them, and re-layouts: 3.71 us -> 4.55 us
where the time goes in v3:
time: 84.6 us; the launch traced here: 84.3 us
  Pallas kernels  77.7 us (92%)
  local copies, waits for them, and re-layouts  6.03 us (7%)
    pallas_call x1, Pallas kernels, shards(): pl.pallas_call(functools.partial(kernel, n_lon, n_lat, slots, lat_cells,...  77.7 us
    unnamed x17, local copies, waits for them, and re-layouts  4.55 us

profile of v3, /device:TPU:0, one launch (start us, length us, event | category | flops | bytes accessed | tf_op | source)
XLA Modules:
  0.0 84.3 jit_solution(15196243446699421692)
XLA Ops:
  0.0 0.8 copy.14
  0.8 0.3 broadcast_in_dim.16
  1.1 0.0 copy-start.6
  1.1 0.2 broadcast_in_dim.17
  1.3 0.5 copy-done.6
  1.8 0.1 copy.13
  1.9 0.3 lt.17
  2.2 0.2 lt.18
  2.4 0.1 lt_iota.8
  2.5 0.0 copy-start.4
  2.5 0.1 copy.16
  2.6 0.8 copy-done.4
  3.4 0.0 copy-start.5
  3.5 0.1 copy.15
  3.5 0.8 copy-done.5
  4.3 0.0 copy-start
  4.3 0.4 pad_maximum_fusion
  4.7 0.1 rev.3
  4.8 0.1 pad.4
  4.9 0.0 copy-start.1
  4.9 0.0 copy-start.2
  5.0 0.0 copy-start.3
  5.0 0.1 copy.17
  5.1 0.5 copy-done
  5.5 0.3 copy-done.1
  5.8 0.0 copy-done.2
  5.9 0.0 copy-done.3
  5.9 77.7 %shard_map.82 = f32[16,32,128]{2,1,0:T(8,128)S(1)} custom-call(f32[16,16]{1,0:T(8,128)S(1)} %copy-done.3, bf16[7,32,16,128]{3,2,1,0:T(8,128)(2,1)S(1)} %copy-done, bf16[2,32,16,128]{3,2,1,0:T(8,128)(2,1)S(1)} %bitcast.7, f32[4,32,128]{2,1,0:T(8,128)S(1)} %copy-done.1, f32[4,32,128]{2,1,0:T(8,128)S(1)} %copy-done.2), custom_call_target="tpu_custom_call" | custom-call | tf_op jit(solution)/shard_map/pallas_call | solution.py:340
  83.6 0.7 copy.19
  (3 shorter events, 0.0 us)
Async XLA Ops:
  1.1 0.7 copy-start.6
  2.5 0.9 %copy-start.4 = (s32[7,32,128]{2,1,0:T(8,128)S(1)}, s32[7,32,128]{2,1,0:T(8,128)}, u32[]{:S(2)}) copy-start(s32[7,32,128]{2,1,0:T(8,128)} %param.10) | copy-start | bytes 344068
  3.4 0.9 %copy-start.5 = (bf16[7,32,2,128]{3,2,1,0:T(2,128)(2,1)S(1)}, bf16[7,32,2,128]{3,2,1,0:T(2,128)(2,1)}, u32[]{:S(2)}) copy-start(bf16[7,32,2,128]{3,2,1,0:T(2,128)(2,1)} %param.9) | copy-start | bytes 344068
  4.3 1.2 %copy-start = (bf16[7,32,16,128]{3,2,1,0:T(8,128)(2,1)S(1)}, bf16[7,32,16,128]{3,2,1,0:T(8,128)(2,1)}, u32[]{:S(2)}) copy-start(bf16[7,32,16,128]{3,2,1,0:T(8,128)(2,1)} %innov_ref.1) | copy-start | bytes 2752516
  4.9 0.9 %copy-start.1 = (f32[4,32,128]{2,1,0:T(8,128)S(1)}, f32[4,32,128]{2,1,0:T(8,128)}, u32[]{:S(2)}) copy-start(f32[4,32,128]{2,1,0:T(8,128)} %u_ref.1) | copy-start | bytes 196612
  4.9 0.9 %copy-start.2 = (f32[4,32,128]{2,1,0:T(8,128)S(1)}, f32[4,32,128]{2,1,0:T(8,128)}, u32[]{:S(2)}) copy-start(f32[4,32,128]{2,1,0:T(8,128)} %v_ref.1) | copy-start | bytes 196612
  5.0 0.9 %copy-start.3 = (f32[16,16]{1,0:T(8,128)S(1)}, f32[16,16]{1,0:T(8,128)}, u32[]{:S(2)}) copy-start(f32[16,16]{1,0:T(8,128)} %mix_ref.1) | copy-start | bytes 3076

commit v4 on v3

--- a/solution.py
+++ b/solution.py
@@ -14,7 +14,7 @@
 KAPPA = 0.125
 EDGE = 8
 GROUP = 4
-AHEAD = 2
+WAVES = 3
 MESH = pl.DeviceIdType.MESH
 
 
@@ -32,7 +32,8 @@
     span = GROUP * width
     tall = lat_cells + 2 * EDGE
     low, high = EDGE, EDGE + lat_cells
-    metas = got_meta.shape[0]
+    cuts = [slots - (slots * w + WAVES - 1) // WAVES for w in range(WAVES + 1)]
+    waves = [(end, first) for first, end in zip(cuts, cuts[1:])]
 
     lat_up = (my_lon, (my_lat + 1) % n_lat)
     lat_down = (my_lon, (my_lat + n_lat - 1) % n_lat)
@@ -47,7 +48,7 @@
         pl.semaphore_signal(barrier, inc=1, device_id=(to // n_lat, to % n_lat), device_id_type=MESH)
 
     own_a = pltpu.make_async_copy(innov_ref.at[:, me], got_innov.at[:, 0], own_sem.at[0])
-    own_b = pltpu.make_async_copy(meta_ref.at[:, me], got_meta.at[:, 0], own_sem.at[1])
+    own_b = pltpu.make_async_copy(meta_ref.at[me], got_meta.at[0], own_sem.at[1])
     own_a.start()
     own_b.start()
     wind[0:LEV, low:high, 0:lon_cells] = u_ref[...]
@@ -109,45 +110,53 @@
     def field_lon(s):
         return lon_pair(lon_send.at[s], lon_got.at[s], flon_send.at[s], flon_recv.at[s])
 
-    def send_slot(s):
-        @pl.loop(1, devices)
-        def _(k):
-            to = (me + k) % devices
-            pltpu.make_async_remote_copy(
-                src_ref=innov_ref.at[s, to], dst_ref=got_innov.at[s, k],
-                send_sem=innov_send.at[s], recv_sem=innov_recv.at[s],
-                device_id=(to // n_lat, to % n_lat), device_id_type=MESH,
-            ).start()
-
-    def slot_total(s):
+    def wave(w, k, to):
+        first, end = waves[w]
         return pltpu.make_async_remote_copy(
-            src_ref=got_innov.at[s, 1:devices], dst_ref=got_innov.at[s, 1:devices],
-            send_sem=innov_send.at[s], recv_sem=innov_recv.at[s], device_id=lat_up, device_id_type=MESH,
-        )
-
-    def send_meta(m):
-        @pl.loop(1, devices)
-        def _(k):
-            to = (me + k) % devices
-            pltpu.make_async_remote_copy(
-                src_ref=meta_ref.at[m, to], dst_ref=got_meta.at[m, k],
-                send_sem=meta_send.at[m], recv_sem=meta_recv.at[m],
-                device_id=(to // n_lat, to % n_lat), device_id_type=MESH,
-            ).start()
-
-    def meta_total(m):
+            src_ref=innov_ref.at[first:end, to], dst_ref=got_innov.at[first:end, k],
+            send_sem=innov_send.at[w], recv_sem=innov_recv.at[w],
+            device_id=(to // n_lat, to % n_lat), device_id_type=MESH,
+        )
+
+    def wave_total(w):
+        first, end = waves[w]
+        whole = got_innov.at[first:end, 1:devices]
         return pltpu.make_async_remote_copy(
-            src_ref=got_meta.at[m, 1:devices], dst_ref=got_meta.at[m, 1:devices],
-            send_sem=meta_send.at[m], recv_sem=meta_recv.at[m], device_id=lat_up, device_id_type=MESH,
+            src_ref=whole, dst_ref=whole,
+            send_sem=innov_send.at[w], recv_sem=innov_recv.at[w], device_id=lat_up, device_id_type=MESH,
+        )
+
+    def meta_copy(k, to):
+        return pltpu.make_async_remote_copy(
+            src_ref=meta_ref.at[to], dst_ref=got_meta.at[k],
+            send_sem=meta_send.at[0], recv_sem=meta_recv.at[0],
+            device_id=(to // n_lat, to % n_lat), device_id_type=MESH,
+        )
+
+    def meta_total():
+        whole = got_meta.at[1:devices]
+        return pltpu.make_async_remote_copy(
+            src_ref=whole, dst_ref=whole,
+            send_sem=meta_send.at[0], recv_sem=meta_recv.at[0], device_id=lat_up, device_id_type=MESH,
         )
 
     wind_lat = lat_pair(wind, wlat_send, wlat_recv)
     wind_lon = lon_pair(wind_send, wind_got, wlon_send, wlon_recv)
     for copy in wind_lat:
         copy.start()
-    send_meta(0)
-    for n in range(AHEAD):
-        send_slot(slots - 1 - n)
+
+    @pl.loop(1, devices)
+    def _(k):
+        to = (me + k) % devices
+        meta_copy(k, to).start()
+        wave(0, k, to).start()
+
+    for w in range(1, len(waves)):
+
+        @pl.loop(1, devices)
+        def _(k):
+            wave(w, k, (me + k) % devices).start()
+
     own_a.wait()
     own_b.wait()
     for copy in wind_lat:
@@ -182,17 +191,15 @@
             + pltpu.roll(near - northward, 1, 0)
         )
 
-    def take_meta(m):
-        meta_total(m).wait_recv()
+    def take_meta():
+        meta_total().wait_recv()
 
         @pl.loop(0, devices // GROUP)
         def _(g):
             for i in range(GROUP):
-                numbers = got_meta[m, g * GROUP + i].astype(jnp.float32)
-                for j in range(4):
-                    s = slots - 1 - (4 * m + j)
-                    if s >= 0:
-                        rows_buf[s, g, 0:4, i * width : (i + 1) * width] = numbers[4 * j : 4 * j + 4]
+                numbers = got_meta[g * GROUP + i].astype(jnp.float32)
+                for s in range(slots):
+                    rows_buf[s, g, 0:4, i * width : (i + 1) * width] = numbers[4 * s : 4 * s + 4]
 
     def gather_slot(s):
         acc[...] = jnp.zeros(acc.shape, jnp.float32)
@@ -247,9 +254,34 @@
         whole = jnp.stack(strips, axis=0)
         field[s, :, low:high, 0:lon_cells] = jnp.swapaxes(whole, 0, 1)
 
+    def settle(s):
+        for copy in field_lon(s):
+            copy.wait_recv()
+        unpack(lon_got.at[s], CH, field.at[s])
+
+        @pl.when(s < slots - 1)
+        def _():
+            @pl.loop(0, CH)
+            def _(c):
+                field[s, c] += stepped(s + 1, c)
+
+    take_meta()
+
     @pl.loop(0, slots)
     def _(n):
         s = slots - 1 - n
+        for w, (_, end) in enumerate(waves):
+
+            @pl.when(s == end - 1)
+            def _():
+                wave_total(w).wait_recv()
+
+        gather_slot(s)
+
+        @pl.when(s > 0)
+        def _():
+            for copy in field_lat(s):
+                copy.start()
 
         @pl.when(n >= 1)
         def _():
@@ -259,64 +291,30 @@
             for copy in field_lon(s + 1):
                 copy.start()
 
-        slot_total(s).wait_recv()
-
-        @pl.when(n + AHEAD < slots)
-        def _():
-            send_slot(s - AHEAD)
-
-        for m in range(1, metas):
-
-            @pl.when(n + AHEAD == 4 * m)
-            def _():
-                send_meta(m)
-
-        for m in range(metas):
-
-            @pl.when(n == 4 * m)
-            def _():
-                take_meta(m)
-
-        gather_slot(s)
-
-        @pl.when(n < slots - 1)
-        def _():
-            for copy in field_lat(s):
-                copy.start()
-
         @pl.when(n == 1)
         def _():
             for copy in wind_lon:
                 copy.wait()
             unpack(wind_got, 2 * LEV, wind)
 
-        @pl.when(n >= 1)
-        def _():
-            for copy in field_lon(s + 1):
-                copy.wait_recv()
-            unpack(lon_got.at[s + 1], CH, field.at[s + 1])
-
         @pl.when(n >= 2)
         def _():
-            @pl.loop(0, CH)
-            def _(c):
-                field[s + 1, c] += stepped(s + 2, c)
+            settle(s + 2)
+
+    settle(1)
 
     @pl.loop(0, CH)
     def _(c):
         out_ref[c] = stepped(1, c)[low:high, 0:lon_cells] + field[0, c, low:high, 0:lon_cells]
 
-    @pl.loop(0, slots)
+    @pl.loop(1, slots)
     def _(s):
-        slot_total(s).wait_send()
-
-        @pl.when(s > 0)
-        def _():
-            for copy in field_lon(s):
-                copy.wait_send()
-
-    for m in range(metas):
-        meta_total(m).wait_send()
+        for copy in field_lon(s):
+            copy.wait_send()
+
+    for w in range(len(waves)):
+        wave_total(w).wait_send()
+    meta_total().wait_send()
 
 
 def shards(n_lon, n_lat, innovations, fractions, cell_index, counts, blocks, u_wind, v_wind, channel_mix):
@@ -329,10 +327,9 @@
     block = jnp.where(live, blocks[..., None], -1).reshape(slots, devices, width)
     places = jnp.stack([cell_index, block], axis=2).astype(jnp.bfloat16)
     meta = jnp.concatenate([fractions, places], axis=2)
-    metas = -(-slots // 4)
-    meta = jnp.pad(meta[::-1], ((0, 4 * metas - slots), (0, 0), (0, 0), (0, 0)))
-    meta = meta.reshape(metas, 4, devices, 4, width)
-    meta = jnp.transpose(meta, (0, 2, 1, 3, 4)).reshape(metas, devices, 16, width)
+    meta = jnp.transpose(meta, (1, 0, 2, 3)).reshape(devices, 4 * slots, width)
+    meta_rows = -(-4 * slots // 16) * 16
+    meta = jnp.pad(meta, ((0, 0), (0, meta_rows - 4 * slots), (0, 0)))
 
     tall, wide = lat_cells + 2 * EDGE, 2 * lon_cells
     f32, bf16, dma = jnp.float32, jnp.bfloat16, pltpu.SemaphoreType.DMA
@@ -350,7 +347,7 @@
         out_specs=vmem,
         scratch_shapes=[
             pltpu.VMEM((slots, devices, channels, width), bf16),
-            pltpu.VMEM((metas, devices, 16, width), bf16),
+            pltpu.VMEM((devices, meta_rows, width), bf16),
             pltpu.VMEM((slots, devices // GROUP, 8, GROUP * width), f32),
             pltpu.VMEM((TILE * TILE, CH * lat_cells * lon_cells // TILE**2), f32),
             pltpu.VMEM((slots, CH, tall, wide), f32),
@@ -360,10 +357,10 @@
             pltpu.VMEM((slots, 2, tall, lon_cells), f32),
             pltpu.VMEM((slots, 2, tall, lon_cells), f32),
             dma((2,)),
-            dma((slots,)),
-            dma((slots,)),
-            dma((metas,)),
-            dma((metas,)),
+            dma((WAVES,)),
+            dma((WAVES,)),
+            dma((1,)),
+            dma((1,)),
             dma((2,)),
             dma((2,)),
             dma((2,)),

time: 84.6 us -> 78.9 us (0.933)
  Pallas kernels: 77.7 us -> 73.3 us
  local copies, waits for them, and re-layouts: 6.03 us -> 5.15 us
    pallas_call x1, Pallas kernels: 77.7 us -> 73.3 us  [shards(): pl.pallas_call(functools.partial(kernel, n_lon, n_lat, slots, lat_cells,...]
    unnamed x17 -> x18, local copies, waits for them, and re-layouts: 4.55 us -> 4 us
where the time goes in v4:
time: 78.9 us; the launch traced here: 78.6 us
  Pallas kernels  73.3 us (93%)
  local copies, waits for them, and re-layouts  5.15 us (7%)
    pallas_call x1, Pallas kernels, shards(): pl.pallas_call(functools.partial(kernel, n_lon, n_lat, slots, lat_cells,...  73.3 us
    unnamed x18, local copies, waits for them, and re-layouts  4 us

profile of v4, /device:TPU:0, one launch (start us, length us, event | category | flops | bytes accessed | tf_op | source)
XLA Modules:
  0.0 78.6 jit_solution(548287146638834950)
XLA Ops:
  0.0 0.8 %copy.14 = s32[7,32,2]{2,1,0:T(8,128)S(1)} copy(s32[7,32,2]{1,2,0:T(2,128)} %param.12) | data formatting | bytes 3584 | tf_op args[4]
  0.8 0.3 broadcast_in_dim.16
  1.1 0.0 copy-start.6
  1.1 0.2 broadcast_in_dim.17
  1.3 0.5 copy-done.6
  1.8 0.1 copy.13
  1.9 0.3 lt.17
  2.2 0.2 lt.18
  2.4 0.1 lt_iota.8
  2.5 0.0 copy-start.4
  2.5 0.0 copy-start.5
  2.5 0.9 %copy-done.4 = bf16[7,32,2,128]{3,2,1,0:T(2,128)(2,1)S(1)} copy-done((bf16[7,32,2,128]{3,2,1,0:T(2,128)(2,1)S(1)}, bf16[7,32,2,128]{3,2,1,0:T(2,128)(2,1)}, u32[]{:S(2)}) %copy-start.4) | copy-done | bytes 114712
  3.4 0.0 copy-start
  3.4 0.0 copy-done.5
  3.5 0.1 copy.17
  3.6 0.0 copy-start.1
  3.6 0.0 copy-start.2
  3.6 0.0 copy-start.3
  3.7 0.9 %copy-done = bf16[7,32,16,128]{3,2,1,0:T(8,128)(2,1)S(1)} copy-done((bf16[7,32,16,128]{3,2,1,0:T(8,128)(2,1)S(1)}, bf16[7,32,16,128]{3,2,1,0:T(8,128)(2,1)}, u32[]{:S(2)}) %copy-start) | copy-done | bytes 917528
  4.6 0.0 copy-done.1
  4.6 0.0 copy-done.2
  4.6 0.0 copy-done.3
  4.6 73.3 %shard_map.82 = f32[16,32,128]{2,1,0:T(8,128)S(1)} custom-call(f32[16,16]{1,0:T(8,128)S(1)} %copy-done.3, bf16[7,32,16,128]{3,2,1,0:T(8,128)(2,1)S(1)} %copy-done, bf16[32,32,128]{2,1,0:T(8,128)(2,1)S(1)} %pad.4.meta_ref, f32[4,32,128]{2,1,0:T(8,128)S(1)} %copy-done.1, f32[4,32,128]{2,1,0:T(8,128)S(1)} %copy-done.2), custom_call_target="tpu_custom_call" | custom-call | tf_op jit(solution)/shard_map/pallas_call | solution.py:337
  77.9 0.7 copy.19
  (6 shorter events, 0.1 us)
Async XLA Ops:
  1.1 0.7 copy-start.6
  2.5 0.9 %copy-start.4 = (bf16[7,32,2,128]{3,2,1,0:T(2,128)(2,1)S(1)}, bf16[7,32,2,128]{3,2,1,0:T(2,128)(2,1)}, u32[]{:S(2)}) copy-start(bf16[7,32,2,128]{3,2,1,0:T(2,128)(2,1)} %param.9) | copy-start | bytes 344068
  2.5 1.0 %copy-start.5 = (s32[7,32,128]{2,1,0:T(8,128)S(1)}, s32[7,32,128]{2,1,0:T(8,128)}, u32[]{:S(2)}) copy-start(s32[7,32,128]{2,1,0:T(8,128)} %param.10) | copy-start | bytes 344068
  3.4 1.2 %copy-start = (bf16[7,32,16,128]{3,2,1,0:T(8,128)(2,1)S(1)}, bf16[7,32,16,128]{3,2,1,0:T(8,128)(2,1)}, u32[]{:S(2)}) copy-start(bf16[7,32,16,128]{3,2,1,0:T(8,128)(2,1)} %innov_ref.1) | copy-start | bytes 2752516
  3.6 1.0 %copy-start.1 = (f32[4,32,128]{2,1,0:T(8,128)S(1)}, f32[4,32,128]{2,1,0:T(8,128)}, u32[]{:S(2)}) copy-start(f32[4,32,128]{2,1,0:T(8,128)} %u_ref.1) | copy-start | bytes 196612
  3.6 1.0 %copy-start.2 = (f32[4,32,128]{2,1,0:T(8,128)S(1)}, f32[4,32,128]{2,1,0:T(8,128)}, u32[]{:S(2)}) copy-start(f32[4,32,128]{2,1,0:T(8,128)} %v_ref.1) | copy-start | bytes 196612
  3.6 1.0 %copy-start.3 = (f32[16,16]{1,0:T(8,128)S(1)}, f32[16,16]{1,0:T(8,128)}, u32[]{:S(2)}) copy-start(f32[16,16]{1,0:T(8,128)} %mix_ref.1) | copy-start | bytes 3076

commit v5 on v4

--- a/solution.py
+++ b/solution.py
@@ -13,7 +13,8 @@
 TILE = 16
 KAPPA = 0.125
 EDGE = 8
-GROUP = 4
+GROUP = 8
+SIDE = 2
 WAVES = 3
 MESH = pl.DeviceIdType.MESH
 
@@ -32,7 +33,7 @@
     span = GROUP * width
     tall = lat_cells + 2 * EDGE
     low, high = EDGE, EDGE + lat_cells
-    cuts = [slots - (slots * w + WAVES - 1) // WAVES for w in range(WAVES + 1)]
+    cuts = [slots] + [(slots - 1) * w // (WAVES - 1) for w in range(WAVES - 1, -1, -1)]
     waves = [(end, first) for first, end in zip(cuts, cuts[1:])]
 
     lat_up = (my_lon, (my_lat + 1) % n_lat)
@@ -51,8 +52,8 @@
     own_b = pltpu.make_async_copy(meta_ref.at[me], got_meta.at[0], own_sem.at[1])
     own_a.start()
     own_b.start()
-    wind[0:LEV, low:high, 0:lon_cells] = u_ref[...]
-    wind[LEV : 2 * LEV, low:high, 0:lon_cells] = v_ref[...]
+    wind[0:LEV, low:high, 0:lon_cells] = 0.5 * u_ref[...]
+    wind[LEV : 2 * LEV, low:high, 0:lon_cells] = 0.5 * v_ref[...]
     pl.semaphore_wait(barrier, devices - 1)
 
     def lat_pair(buffer, send, recv):
@@ -174,22 +175,32 @@
     last_row = jnp.where(my_lat == n_lat - 1, high, tall)
     inside = (row_at >= first_row) & (row_at < last_row)
 
-    def stepped(older, c):
-        total = mix_ref[0, c] * field[older, 0]
+    def stepped(older, channels):
+        below = field[older, 0]
+        totals = [mix_ref[0, c] * below for c in channels]
         for d in range(1, CH):
-            total = total + mix_ref[d, c] * field[older, d]
-        total = jnp.where(inside, total, 0.0)
-        level = c % LEV
-        eastward = (0.5 * wind[level]) * total
-        northward = (0.5 * wind[LEV + level]) * total
-        near = KAPPA * total
-        return (
-            (1.0 - 4.0 * KAPPA) * total
-            + pltpu.roll(near + eastward, 2 * lon_cells - 1, 1)
-            + pltpu.roll(near - eastward, 1, 1)
-            + pltpu.roll(near + northward, tall - 1, 0)
-            + pltpu.roll(near - northward, 1, 0)
-        )
+            below = field[older, d]
+            totals = [total + mix_ref[d, c] * below for c, total in zip(channels, totals)]
+        level = channels[0] % LEV
+        half_u, half_v = wind[level], wind[LEV + level]
+        results = []
+        for total in totals:
+            total = jnp.where(inside, total, 0.0)
+            eastward = half_u * total
+            northward = half_v * total
+            near = KAPPA * total
+            results.append(
+                (1.0 - 4.0 * KAPPA) * total
+                + pltpu.roll(near + eastward, 2 * lon_cells - 1, 1)
+                + pltpu.roll(near - eastward, 1, 1)
+                + pltpu.roll(near + northward, tall - 1, 0)
+                + pltpu.roll(near - northward, 1, 0)
+            )
+        return results
+
+    def same_level(i):
+        first = (i // LEV) * LEV * SIDE + i % LEV
+        return [first + LEV * j for j in range(SIDE)]
 
     def take_meta():
         meta_total().wait_recv()
@@ -261,9 +272,12 @@
 
         @pl.when(s < slots - 1)
         def _():
-            @pl.loop(0, CH)
-            def _(c):
-                field[s, c] += stepped(s + 1, c)
+            @pl.loop(0, CH // SIDE)
+            def _(i):
+                channels = same_level(i)
+                news = [new + field[s, c] for c, new in zip(channels, stepped(s + 1, channels))]
+                for c, new in zip(channels, news):
+                    field[s, c] = new
 
     take_meta()
 
@@ -303,9 +317,11 @@
 
     settle(1)
 
-    @pl.loop(0, CH)
-    def _(c):
-        out_ref[c] = stepped(1, c)[low:high, 0:lon_cells] + field[0, c, low:high, 0:lon_cells]
+    @pl.loop(0, CH // SIDE)
+    def _(i):
+        channels = same_level(i)
+        for c, new in zip(channels, stepped(1, channels)):
+            out_ref[c] = new[low:high, 0:lon_cells] + field[0, c, low:high, 0:lon_cells]
 
     @pl.loop(1, slots)
     def _(s):

time: 78.9 us -> 70.8 us (0.90)
  Pallas kernels: 73.3 us -> 65.3 us
    pallas_call x1, Pallas kernels: 73.3 us -> 65.3 us  [shards(): pl.pallas_call(functools.partial(kernel, n_lon, n_lat, slots, lat_cells,...]
where the time goes in v5:
time: 70.8 us; the launch traced here: 70.6 us
  Pallas kernels  65.3 us (92%)
  local copies, waits for them, and re-layouts  5.15 us (7%)
    pallas_call x1, Pallas kernels, shards(): pl.pallas_call(functools.partial(kernel, n_lon, n_lat, slots, lat_cells,...  65.3 us
    unnamed x18, local copies, waits for them, and re-layouts  4 us

profile of v5, /device:TPU:0, one launch (start us, length us, event | category | flops | bytes accessed | tf_op | source)
XLA Modules:
  0.0 70.6 jit_solution(11883609347008911040)
XLA Ops:
  0.0 0.8 %copy.14 = s32[7,32,2]{2,1,0:T(8,128)S(1)} copy(s32[7,32,2]{1,2,0:T(2,128)} %param.12) | data formatting | bytes 3584 | tf_op args[4]
  0.8 0.3 broadcast_in_dim.16
  1.1 0.0 copy-start.6
  1.1 0.2 broadcast_in_dim.17
  1.3 0.5 copy-done.6
  1.8 0.1 copy.13
  1.9 0.3 lt.17
  2.2 0.2 lt.18
  2.4 0.1 lt_iota.8
  2.5 0.0 copy-start.4
  2.5 0.0 copy-start.5
  2.5 0.9 %copy-done.4 = bf16[7,32,2,128]{3,2,1,0:T(2,128)(2,1)S(1)} copy-done((bf16[7,32,2,128]{3,2,1,0:T(2,128)(2,1)S(1)}, bf16[7,32,2,128]{3,2,1,0:T(2,128)(2,1)}, u32[]{:S(2)}) %copy-start.4) | copy-done | bytes 114712
  3.4 0.0 copy-start
  3.4 0.0 copy-done.5
  3.5 0.1 copy.17
  3.6 0.0 copy-start.1
  3.6 0.0 copy-start.2
  3.6 0.0 copy-start.3
  3.7 0.9 %copy-done = bf16[7,32,16,128]{3,2,1,0:T(8,128)(2,1)S(1)} copy-done((bf16[7,32,16,128]{3,2,1,0:T(8,128)(2,1)S(1)}, bf16[7,32,16,128]{3,2,1,0:T(8,128)(2,1)}, u32[]{:S(2)}) %copy-start) | copy-done | bytes 917528
  4.6 0.0 copy-done.1
  4.6 0.0 copy-done.2
  4.6 0.0 copy-done.3
  4.6 65.3 %shard_map.82 = f32[16,32,128]{2,1,0:T(8,128)S(1)} custom-call(f32[16,16]{1,0:T(8,128)S(1)} %copy-done.3, bf16[7,32,16,128]{3,2,1,0:T(8,128)(2,1)S(1)} %copy-done, bf16[32,32,128]{2,1,0:T(8,128)(2,1)S(1)} %pad.4.meta_ref, f32[4,32,128]{2,1,0:T(8,128)S(1)} %copy-done.1, f32[4,32,128]{2,1,0:T(8,128)S(1)} %copy-done.2), custom_call_target="tpu_custom_call" | custom-call | tf_op jit(solution)/shard_map/pallas_call | solution.py:353
  69.9 0.7 copy.19
  (6 shorter events, 0.1 us)
Async XLA Ops:
  1.1 0.7 copy-start.6
  2.5 0.9 %copy-start.4 = (bf16[7,32,2,128]{3,2,1,0:T(2,128)(2,1)S(1)}, bf16[7,32,2,128]{3,2,1,0:T(2,128)(2,1)}, u32[]{:S(2)}) copy-start(bf16[7,32,2,128]{3,2,1,0:T(2,128)(2,1)} %param.9) | copy-start | bytes 344068
  2.5 1.0 %copy-start.5 = (s32[7,32,128]{2,1,0:T(8,128)S(1)}, s32[7,32,128]{2,1,0:T(8,128)}, u32[]{:S(2)}) copy-start(s32[7,32,128]{2,1,0:T(8,128)} %param.10) | copy-start | bytes 344068
  3.4 1.2 %copy-start = (bf16[7,32,16,128]{3,2,1,0:T(8,128)(2,1)S(1)}, bf16[7,32,16,128]{3,2,1,0:T(8,128)(2,1)}, u32[]{:S(2)}) copy-start(bf16[7,32,16,128]{3,2,1,0:T(8,128)(2,1)} %innov_ref.1) | copy-start | bytes 2752516
  3.6 1.0 %copy-start.1 = (f32[4,32,128]{2,1,0:T(8,128)S(1)}, f32[4,32,128]{2,1,0:T(8,128)}, u32[]{:S(2)}) copy-start(f32[4,32,128]{2,1,0:T(8,128)} %u_ref.1) | copy-start | bytes 196612
  3.6 1.0 %copy-start.2 = (f32[4,32,128]{2,1,0:T(8,128)S(1)}, f32[4,32,128]{2,1,0:T(8,128)}, u32[]{:S(2)}) copy-start(f32[4,32,128]{2,1,0:T(8,128)} %v_ref.1) | copy-start | bytes 196612
  3.6 1.0 %copy-start.3 = (f32[16,16]{1,0:T(8,128)S(1)}, f32[16,16]{1,0:T(8,128)}, u32[]{:S(2)}) copy-start(f32[16,16]{1,0:T(8,128)} %mix_ref.1) | copy-start | bytes 3076

commit v6 on v5

--- a/solution.py
+++ b/solution.py
@@ -15,7 +15,7 @@
 EDGE = 8
 GROUP = 8
 SIDE = 2
-WAVES = 3
+WAVE = 2
 MESH = pl.DeviceIdType.MESH
 
 
@@ -33,8 +33,11 @@
     span = GROUP * width
     tall = lat_cells + 2 * EDGE
     low, high = EDGE, EDGE + lat_cells
-    cuts = [slots] + [(slots - 1) * w // (WAVES - 1) for w in range(WAVES - 1, -1, -1)]
-    waves = [(end, first) for first, end in zip(cuts, cuts[1:])]
+    waves = [(slots - 1, slots)]
+    while waves[-1][0] > 0:
+        end = waves[-1][0]
+        waves.append((max(end - WAVE, 0), end))
+    metas = got_meta.shape[0]
 
     lat_up = (my_lon, (my_lat + 1) % n_lat)
     lat_down = (my_lon, (my_lat + n_lat - 1) % n_lat)
@@ -49,7 +52,7 @@
         pl.semaphore_signal(barrier, inc=1, device_id=(to // n_lat, to % n_lat), device_id_type=MESH)
 
     own_a = pltpu.make_async_copy(innov_ref.at[:, me], got_innov.at[:, 0], own_sem.at[0])
-    own_b = pltpu.make_async_copy(meta_ref.at[me], got_meta.at[0], own_sem.at[1])
+    own_b = pltpu.make_async_copy(meta_ref.at[:, me], got_meta.at[:, 0], own_sem.at[1])
     own_a.start()
     own_b.start()
     wind[0:LEV, low:high, 0:lon_cells] = 0.5 * u_ref[...]
@@ -127,18 +130,18 @@
             send_sem=innov_send.at[w], recv_sem=innov_recv.at[w], device_id=lat_up, device_id_type=MESH,
         )
 
-    def meta_copy(k, to):
+    def meta_copy(m, k, to):
         return pltpu.make_async_remote_copy(
-            src_ref=meta_ref.at[to], dst_ref=got_meta.at[k],
-            send_sem=meta_send.at[0], recv_sem=meta_recv.at[0],
+            src_ref=meta_ref.at[m, to], dst_ref=got_meta.at[m, k],
+            send_sem=meta_send.at[m], recv_sem=meta_recv.at[m],
             device_id=(to // n_lat, to % n_lat), device_id_type=MESH,
         )
 
-    def meta_total():
-        whole = got_meta.at[1:devices]
+    def meta_total(m):
+        whole = got_meta.at[m, 1:devices]
         return pltpu.make_async_remote_copy(
             src_ref=whole, dst_ref=whole,
-            send_sem=meta_send.at[0], recv_sem=meta_recv.at[0], device_id=lat_up, device_id_type=MESH,
+            send_sem=meta_send.at[m], recv_sem=meta_recv.at[m], device_id=lat_up, device_id_type=MESH,
         )
 
     wind_lat = lat_pair(wind, wlat_send, wlat_recv)
@@ -146,18 +149,19 @@
     for copy in wind_lat:
         copy.start()
 
-    @pl.loop(1, devices)
-    def _(k):
-        to = (me + k) % devices
-        meta_copy(k, to).start()
-        wave(0, k, to).start()
-
-    for w in range(1, len(waves)):
-
+    def send_wave(w):
         @pl.loop(1, devices)
         def _(k):
-            wave(w, k, (me + k) % devices).start()
-
+            to = (me + k) % devices
+            if w == 0:
+                meta_copy(0, k, to).start()
+            if w == 2:
+                for m in range(1, metas):
+                    meta_copy(m, k, to).start()
+            wave(w, k, to).start()
+
+    send_wave(0)
+    send_wave(1)
     own_a.wait()
     own_b.wait()
     for copy in wind_lat:
@@ -202,15 +206,17 @@
         first = (i // LEV) * LEV * SIDE + i % LEV
         return [first + LEV * j for j in range(SIDE)]
 
-    def take_meta():
-        meta_total().wait_recv()
+    def take_meta(m):
+        meta_total(m).wait_recv()
 
         @pl.loop(0, devices // GROUP)
         def _(g):
             for i in range(GROUP):
-                numbers = got_meta[g * GROUP + i].astype(jnp.float32)
-                for s in range(slots):
-                    rows_buf[s, g, 0:4, i * width : (i + 1) * width] = numbers[4 * s : 4 * s + 4]
+                numbers = got_meta[m, g * GROUP + i].astype(jnp.float32)
+                for j in range(4):
+                    s = slots - 1 - (4 * m + j)
+                    if s >= 0:
+                        rows_buf[s, g, 0:4, i * width : (i + 1) * width] = numbers[4 * j : 4 * j + 4]
 
     def gather_slot(s):
         acc[...] = jnp.zeros(acc.shape, jnp.float32)
@@ -279,8 +285,6 @@
                 for c, new in zip(channels, news):
                     field[s, c] = new
 
-    take_meta()
-
     @pl.loop(0, slots)
     def _(n):
         s = slots - 1 - n
@@ -289,6 +293,12 @@
             @pl.when(s == end - 1)
             def _():
                 wave_total(w).wait_recv()
+
+        for m in range(metas):
+
+            @pl.when(n == 4 * m)
+            def _():
+                take_meta(m)
 
         gather_slot(s)
 
@@ -305,6 +315,12 @@
             for copy in field_lon(s + 1):
                 copy.start()
 
+        for w in range(2, len(waves)):
+
+            @pl.when(n == WAVE * w - 3)
+            def _():
+                send_wave(w)
+
         @pl.when(n == 1)
         def _():
             for copy in wind_lon:
@@ -330,7 +346,8 @@
 
     for w in range(len(waves)):
         wave_total(w).wait_send()
-    meta_total().wait_send()
+    for m in range(metas):
+        meta_total(m).wait_send()
 
 
 def shards(n_lon, n_lat, innovations, fractions, cell_index, counts, blocks, u_wind, v_wind, channel_mix):
@@ -343,9 +360,10 @@
     block = jnp.where(live, blocks[..., None], -1).reshape(slots, devices, width)
     places = jnp.stack([cell_index, block], axis=2).astype(jnp.bfloat16)
     meta = jnp.concatenate([fractions, places], axis=2)
-    meta = jnp.transpose(meta, (1, 0, 2, 3)).reshape(devices, 4 * slots, width)
-    meta_rows = -(-4 * slots // 16) * 16
-    meta = jnp.pad(meta, ((0, 0), (0, meta_rows - 4 * slots), (0, 0)))
+    metas, waves = -(-slots // 4), 1 - (1 - slots) // WAVE
+    meta = jnp.pad(meta[::-1], ((0, 4 * metas - slots), (0, 0), (0, 0), (0, 0)))
+    meta = meta.reshape(metas, 4, devices, 4, width)
+    meta = jnp.transpose(meta, (0, 2, 1, 3, 4)).reshape(metas, devices, 16, width)
 
     tall, wide = lat_cells + 2 * EDGE, 2 * lon_cells
     f32, bf16, dma = jnp.float32, jnp.bfloat16, pltpu.SemaphoreType.DMA
@@ -363,7 +381,7 @@
         out_specs=vmem,
         scratch_shapes=[
             pltpu.VMEM((slots, devices, channels, width), bf16),
-            pltpu.VMEM((devices, meta_rows, width), bf16),
+            pltpu.VMEM((metas, devices, 16, width), bf16),
             pltpu.VMEM((slots, devices // GROUP, 8, GROUP * width), f32),
             pltpu.VMEM((TILE * TILE, CH * lat_cells * lon_cells // TILE**2), f32),
             pltpu.VMEM((slots, CH, tall, wide), f32),
@@ -373,10 +391,10 @@
             pltpu.VMEM((slots, 2, tall, lon_cells), f32),
             pltpu.VMEM((slots, 2, tall, lon_cells), f32),
             dma((2,)),
-            dma((WAVES,)),
-            dma((WAVES,)),
-            dma((1,)),
-            dma((1,)),
+            dma((waves,)),
+            dma((waves,)),
+            dma((metas,)),
+            dma((metas,)),
             dma((2,)),
             dma((2,)),
             dma((2,)),

time: 70.8 us -> 69.9 us (0.987)
  Pallas kernels: 65.3 us -> 63.1 us
  local copies, waits for them, and re-layouts: 5.15 us -> 6.03 us
    pallas_call x1, Pallas kernels: 65.3 us -> 63.1 us  [shards(): pl.pallas_call(functools.partial(kernel, n_lon, n_lat, slots, lat_cells,...]
    unnamed x18 -> x17, local copies, waits for them, and re-layouts: 4 us -> 4.55 us
where the time goes in v6:
time: 69.9 us; the launch traced here: 69.6 us
  Pallas kernels  63.1 us (90%)
  local copies, waits for them, and re-layouts  6.03 us (9%)
    pallas_call x1, Pallas kernels, shards(): pl.pallas_call(functools.partial(kernel, n_lon, n_lat, slots, lat_cells,...  63.1 us
    unnamed x17, local copies, waits for them, and re-layouts  4.55 us

profile of v6, /device:TPU:0, one launch (start us, length us, event | category | flops | bytes accessed | tf_op | source)
XLA Modules:
  0.0 69.6 jit_solution(14497791220488829929)
XLA Ops:
  0.0 0.8 %copy.14 = s32[7,32,2]{2,1,0:T(8,128)S(1)} copy(s32[7,32,2]{1,2,0:T(2,128)} %param.12) | data formatting | bytes 3584 | tf_op args[4]
  0.8 0.3 broadcast_in_dim.16
  1.1 0.0 copy-start.6
  1.1 0.2 broadcast_in_dim.17
  1.3 0.5 copy-done.6
  1.8 0.1 copy.13
  1.9 0.3 lt.17
  2.2 0.2 lt.18
  2.4 0.1 lt_iota.8
  2.5 0.0 copy-start.4
  2.5 0.1 copy.16
  2.6 0.8 %copy-done.4 = s32[7,32,128]{2,1,0:T(8,128)S(1)} copy-done((s32[7,32,128]{2,1,0:T(8,128)S(1)}, s32[7,32,128]{2,1,0:T(8,128)}, u32[]{:S(2)}) %copy-start.4) | copy-done | bytes 114712
  3.4 0.0 copy-start.5
  3.5 0.1 copy.15
  3.5 0.8 %copy-done.5 = bf16[7,32,2,128]{3,2,1,0:T(2,128)(2,1)S(1)} copy-done((bf16[7,32,2,128]{3,2,1,0:T(2,128)(2,1)S(1)}, bf16[7,32,2,128]{3,2,1,0:T(2,128)(2,1)}, u32[]{:S(2)}) %copy-start.5) | copy-done | bytes 114712
  4.3 0.0 copy-start
  4.3 0.4 pad_maximum_fusion
  4.7 0.1 rev.3
  4.8 0.1 pad.4
  4.9 0.0 copy-start.1
  4.9 0.0 copy-start.2
  5.0 0.0 copy-start.3
  5.0 0.1 copy.17
  5.1 0.5 copy-done
  5.5 0.3 copy-done.1
  5.8 0.0 copy-done.2
  5.9 0.0 copy-done.3
  5.9 63.1 %shard_map.82 = f32[16,32,128]{2,1,0:T(8,128)S(1)} custom-call(f32[16,16]{1,0:T(8,128)S(1)} %copy-done.3, bf16[7,32,16,128]{3,2,1,0:T(8,128)(2,1)S(1)} %copy-done, bf16[2,32,16,128]{3,2,1,0:T(8,128)(2,1)S(1)} %bitcast.7, f32[4,32,128]{2,1,0:T(8,128)S(1)} %copy-done.1, f32[4,32,128]{2,1,0:T(8,128)S(1)} %copy-done.2), custom_call_target="tpu_custom_call" | custom-call | tf_op jit(solution)/shard_map/pallas_call | solution.py:371
  68.9 0.7 %copy.19 = f32[4,4,32,128]{3,2,1,0:T(8,128)} copy(f32[4,4,32,128]{3,2,1,0:T(8,128)S(1)} %bitcast.8) | data formatting | bytes 524288
  (3 shorter events, 0.0 us)
Async XLA Ops:
  1.1 0.7 %copy-start.6 = (s32[7,32,2]{1,2,0:T(2,128)S(1)}, s32[7,32,2]{1,2,0:T(2,128)}, u32[]{:S(2)}) copy-start(s32[7,32,2]{1,2,0:T(2,128)} %param.11) | copy-start | bytes 5380
  2.5 0.9 %copy-start.4 = (s32[7,32,128]{2,1,0:T(8,128)S(1)}, s32[7,32,128]{2,1,0:T(8,128)}, u32[]{:S(2)}) copy-start(s32[7,32,128]{2,1,0:T(8,128)} %param.10) | copy-start | bytes 344068
  3.4 0.9 %copy-start.5 = (bf16[7,32,2,128]{3,2,1,0:T(2,128)(2,1)S(1)}, bf16[7,32,2,128]{3,2,1,0:T(2,128)(2,1)}, u32[]{:S(2)}) copy-start(bf16[7,32,2,128]{3,2,1,0:T(2,128)(2,1)} %param.9) | copy-start | bytes 344068
  4.3 1.2 %copy-start = (bf16[7,32,16,128]{3,2,1,0:T(8,128)(2,1)S(1)}, bf16[7,32,16,128]{3,2,1,0:T(8,128)(2,1)}, u32[]{:S(2)}) copy-start(bf16[7,32,16,128]{3,2,1,0:T(8,128)(2,1)} %innov_ref.1) | copy-start | bytes 2752516
  4.9 0.9 %copy-start.1 = (f32[4,32,128]{2,1,0:T(8,128)S(1)}, f32[4,32,128]{2,1,0:T(8,128)}, u32[]{:S(2)}) copy-start(f32[4,32,128]{2,1,0:T(8,128)} %u_ref.1) | copy-start | bytes 196612
  4.9 0.9 %copy-start.2 = (f32[4,32,128]{2,1,0:T(8,128)S(1)}, f32[4,32,128]{2,1,0:T(8,128)}, u32[]{:S(2)}) copy-start(f32[4,32,128]{2,1,0:T(8,128)} %v_ref.1) | copy-start | bytes 196612
  5.0 0.9 %copy-start.3 = (f32[16,16]{1,0:T(8,128)S(1)}, f32[16,16]{1,0:T(8,128)}, u32[]{:S(2)}) copy-start(f32[16,16]{1,0:T(8,128)} %mix_ref.1) | copy-start | bytes 3076

commit v7 on v6

--- a/solution.py
+++ b/solution.py
@@ -14,7 +14,7 @@
 KAPPA = 0.125
 EDGE = 8
 GROUP = 8
-SIDE = 2
+SIDE = 4
 WAVE = 2
 MESH = pl.DeviceIdType.MESH
 
@@ -225,7 +225,7 @@
         def _(g):
             values = jnp.concatenate(
                 [got_innov[s, g * GROUP + i] for i in range(GROUP)], axis=1
-            )
+            ).astype(jnp.float32)
             frac_y, frac_x = rows_buf[s, g, 0:1], rows_buf[s, g, 1:2]
             cell, block = rows_buf[s, g, 2:3], rows_buf[s, g, 3:4]
             row = jnp.floor(cell * (1.0 / TILE))
@@ -239,10 +239,10 @@
                 heads.append(head)
                 tails.append((weight - head.astype(jnp.float32)).astype(jnp.bfloat16))
             weights = jnp.concatenate(heads + tails, axis=0)
+            blocks = jnp.broadcast_to(block, (CH, span))
             placed = []
             for b in range(lat_cells // TILE * across):
-                here = jnp.broadcast_to(jnp.where(block == float(b), 1.0, 0.0), (CH, span)).astype(jnp.bfloat16)
-                placed.append(values * here)
+                placed.append(jnp.where(blocks == float(b), values, 0.0).astype(jnp.bfloat16))
             placed = jnp.concatenate(placed, axis=0)
             both = lax.dot_general(weights, placed, contract, preferred_element_type=jnp.float32)
             acc[...] += both[: TILE * TILE] + both[TILE * TILE :]
@@ -317,7 +317,7 @@
 
         for w in range(2, len(waves)):
 
-            @pl.when(n == WAVE * w - 3)
+            @pl.when(n == WAVE * w - 4)
             def _():
                 send_wave(w)
 

time: 69.9 us -> 63.2 us (0.904)
  Pallas kernels: 63.1 us -> 56.3 us
    pallas_call x1, Pallas kernels: 63.1 us -> 56.3 us  [shards(): pl.pallas_call(functools.partial(kernel, n_lon, n_lat, slots, lat_cells,...]
where the time goes in v7:
time: 63.2 us; the launch traced here: 62.8 us
  Pallas kernels  56.3 us (89%)
  local copies, waits for them, and re-layouts  6.03 us (10%)
    pallas_call x1, Pallas kernels, shards(): pl.pallas_call(functools.partial(kernel, n_lon, n_lat, slots, lat_cells,...  56.3 us
    unnamed x17, local copies, waits for them, and re-layouts  4.55 us

profile of v7, /device:TPU:0, one launch (start us, length us, event | category | flops | bytes accessed | tf_op | source)
XLA Modules:
  0.0 62.8 jit_solution(4447806256774476037)
XLA Ops:
  0.0 0.8 %copy.14 = s32[7,32,2]{2,1,0:T(8,128)S(1)} copy(s32[7,32,2]{1,2,0:T(2,128)} %param.12) | data formatting | bytes 3584 | tf_op args[4]
  0.8 0.3 broadcast_in_dim.16
  1.1 0.0 copy-start.6
  1.1 0.2 broadcast_in_dim.17
  1.3 0.5 copy-done.6
  1.8 0.1 copy.13
  1.9 0.3 lt.17
  2.2 0.2 lt.18
  2.4 0.1 lt_iota.8
  2.5 0.0 copy-start.4
  2.5 0.1 copy.16
  2.6 0.8 %copy-done.4 = s32[7,32,128]{2,1,0:T(8,128)S(1)} copy-done((s32[7,32,128]{2,1,0:T(8,128)S(1)}, s32[7,32,128]{2,1,0:T(8,128)}, u32[]{:S(2)}) %copy-start.4) | copy-done | bytes 114712
  3.4 0.0 copy-start.5
  3.5 0.1 copy.15
  3.5 0.8 %copy-done.5 = bf16[7,32,2,128]{3,2,1,0:T(2,128)(2,1)S(1)} copy-done((bf16[7,32,2,128]{3,2,1,0:T(2,128)(2,1)S(1)}, bf16[7,32,2,128]{3,2,1,0:T(2,128)(2,1)}, u32[]{:S(2)}) %copy-start.5) | copy-done | bytes 114712
  4.3 0.0 copy-start
  4.3 0.4 pad_maximum_fusion
  4.7 0.1 rev.3
  4.8 0.1 pad.4
  4.9 0.0 copy-start.1
  4.9 0.0 copy-start.2
  5.0 0.0 copy-start.3
  5.0 0.1 copy.17
  5.1 0.5 copy-done
  5.5 0.3 copy-done.1
  5.8 0.0 copy-done.2
  5.9 0.0 copy-done.3
  5.9 56.3 %shard_map.82 = f32[16,32,128]{2,1,0:T(8,128)S(1)} custom-call(f32[16,16]{1,0:T(8,128)S(1)} %copy-done.3, bf16[7,32,16,128]{3,2,1,0:T(8,128)(2,1)S(1)} %copy-done, bf16[2,32,16,128]{3,2,1,0:T(8,128)(2,1)S(1)} %bitcast.7, f32[4,32,128]{2,1,0:T(8,128)S(1)} %copy-done.1, f32[4,32,128]{2,1,0:T(8,128)S(1)} %copy-done.2), custom_call_target="tpu_custom_call" | custom-call | tf_op jit(solution)/shard_map/pallas_call | solution.py:371
  62.1 0.7 %copy.19 = f32[4,4,32,128]{3,2,1,0:T(8,128)} copy(f32[4,4,32,128]{3,2,1,0:T(8,128)S(1)} %bitcast.8) | data formatting | bytes 524288
  (3 shorter events, 0.0 us)
Async XLA Ops:
  1.1 0.7 %copy-start.6 = (s32[7,32,2]{1,2,0:T(2,128)S(1)}, s32[7,32,2]{1,2,0:T(2,128)}, u32[]{:S(2)}) copy-start(s32[7,32,2]{1,2,0:T(2,128)} %param.11) | copy-start | bytes 5380
  2.5 0.9 %copy-start.4 = (s32[7,32,128]{2,1,0:T(8,128)S(1)}, s32[7,32,128]{2,1,0:T(8,128)}, u32[]{:S(2)}) copy-start(s32[7,32,128]{2,1,0:T(8,128)} %param.10) | copy-start | bytes 344068
  3.4 0.9 %copy-start.5 = (bf16[7,32,2,128]{3,2,1,0:T(2,128)(2,1)S(1)}, bf16[7,32,2,128]{3,2,1,0:T(2,128)(2,1)}, u32[]{:S(2)}) copy-start(bf16[7,32,2,128]{3,2,1,0:T(2,128)(2,1)} %param.9) | copy-start | bytes 344068
  4.3 1.2 %copy-start = (bf16[7,32,16,128]{3,2,1,0:T(8,128)(2,1)S(1)}, bf16[7,32,16,128]{3,2,1,0:T(8,128)(2,1)}, u32[]{:S(2)}) copy-start(bf16[7,32,16,128]{3,2,1,0:T(8,128)(2,1)} %innov_ref.1) | copy-start | bytes 2752516
  4.9 0.9 %copy-start.1 = (f32[4,32,128]{2,1,0:T(8,128)S(1)}, f32[4,32,128]{2,1,0:T(8,128)}, u32[]{:S(2)}) copy-start(f32[4,32,128]{2,1,0:T(8,128)} %u_ref.1) | copy-start | bytes 196612
  4.9 0.9 %copy-start.2 = (f32[4,32,128]{2,1,0:T(8,128)S(1)}, f32[4,32,128]{2,1,0:T(8,128)}, u32[]{:S(2)}) copy-start(f32[4,32,128]{2,1,0:T(8,128)} %v_ref.1) | copy-start | bytes 196612
  5.0 0.9 %copy-start.3 = (f32[16,16]{1,0:T(8,128)S(1)}, f32[16,16]{1,0:T(8,128)}, u32[]{:S(2)}) copy-start(f32[16,16]{1,0:T(8,128)} %mix_ref.1) | copy-start | bytes 3076

commit v8 on v7

--- a/solution.py
+++ b/solution.py
@@ -13,7 +13,7 @@
 TILE = 16
 KAPPA = 0.125
 EDGE = 8
-GROUP = 8
+GROUP = 16
 SIDE = 4
 WAVE = 2
 MESH = pl.DeviceIdType.MESH
@@ -162,6 +162,7 @@
 
     send_wave(0)
     send_wave(1)
+    send_wave(2)
     own_a.wait()
     own_b.wait()
     for copy in wind_lat:
@@ -315,9 +316,9 @@
             for copy in field_lon(s + 1):
                 copy.start()
 
-        for w in range(2, len(waves)):
-
-            @pl.when(n == WAVE * w - 4)
+        for w in range(3, len(waves)):
+
+            @pl.when(n == WAVE * w - 5)
             def _():
                 send_wave(w)
 

time: 63.2 us -> 63.9 us (1.011); the launches traced: 62.8 us -> 62.8 us
  no operation moved by 1% of the time
where the time goes in v8:
time: 63.9 us; the launch traced here: 62.8 us
  Pallas kernels  56.2 us (88%)
  local copies, waits for them, and re-layouts  6.03 us (9%)
    pallas_call x1, Pallas kernels, shards(): pl.pallas_call(functools.partial(kernel, n_lon, n_lat, slots, lat_cells,...  56.2 us
    unnamed x17, local copies, waits for them, and re-layouts  4.55 us

profile of v8, /device:TPU:0, one launch (start us, length us, event | category | flops | bytes accessed | tf_op | source)
XLA Modules:
  0.0 62.8 jit_solution(3464768148988369904)
XLA Ops:
  0.0 0.8 %copy.14 = s32[7,32,2]{2,1,0:T(8,128)S(1)} copy(s32[7,32,2]{1,2,0:T(2,128)} %param.12) | data formatting | bytes 3584 | tf_op args[4]
  0.8 0.3 broadcast_in_dim.16
  1.1 0.0 copy-start.6
  1.1 0.2 broadcast_in_dim.17
  1.3 0.5 copy-done.6
  1.8 0.1 copy.13
  1.9 0.3 lt.17
  2.2 0.2 lt.18
  2.4 0.1 lt_iota.8
  2.5 0.0 copy-start.4
  2.5 0.1 copy.16
  2.6 0.8 %copy-done.4 = s32[7,32,128]{2,1,0:T(8,128)S(1)} copy-done((s32[7,32,128]{2,1,0:T(8,128)S(1)}, s32[7,32,128]{2,1,0:T(8,128)}, u32[]{:S(2)}) %copy-start.4) | copy-done | bytes 114712
  3.4 0.0 copy-start.5
  3.5 0.1 copy.15
  3.5 0.8 %copy-done.5 = bf16[7,32,2,128]{3,2,1,0:T(2,128)(2,1)S(1)} copy-done((bf16[7,32,2,128]{3,2,1,0:T(2,128)(2,1)S(1)}, bf16[7,32,2,128]{3,2,1,0:T(2,128)(2,1)}, u32[]{:S(2)}) %copy-start.5) | copy-done | bytes 114712
  4.3 0.0 copy-start
  4.3 0.4 pad_maximum_fusion
  4.7 0.1 rev.3
  4.8 0.1 pad.4
  4.9 0.0 copy-start.1
  4.9 0.0 copy-start.2
  5.0 0.0 copy-start.3
  5.0 0.1 copy.17
  5.1 0.5 copy-done
  5.5 0.3 copy-done.1
  5.8 0.0 copy-done.2
  5.9 0.0 copy-done.3
  5.9 56.2 %shard_map.82 = f32[16,32,128]{2,1,0:T(8,128)S(1)} custom-call(f32[16,16]{1,0:T(8,128)S(1)} %copy-done.3, bf16[7,32,16,128]{3,2,1,0:T(8,128)(2,1)S(1)} %copy-done, bf16[2,32,16,128]{3,2,1,0:T(8,128)(2,1)S(1)} %bitcast.7, f32[4,32,128]{2,1,0:T(8,128)S(1)} %copy-done.1, f32[4,32,128]{2,1,0:T(8,128)S(1)} %copy-done.2), custom_call_target="tpu_custom_call" | custom-call | tf_op jit(solution)/shard_map/pallas_call | solution.py:372
  62.1 0.7 %copy.19 = f32[4,4,32,128]{3,2,1,0:T(8,128)} copy(f32[4,4,32,128]{3,2,1,0:T(8,128)S(1)} %bitcast.8) | data formatting | bytes 524288
  (3 shorter events, 0.0 us)
Async XLA Ops:
  1.1 0.7 %copy-start.6 = (s32[7,32,2]{1,2,0:T(2,128)S(1)}, s32[7,32,2]{1,2,0:T(2,128)}, u32[]{:S(2)}) copy-start(s32[7,32,2]{1,2,0:T(2,128)} %param.11) | copy-start | bytes 5380
  2.5 0.9 %copy-start.4 = (s32[7,32,128]{2,1,0:T(8,128)S(1)}, s32[7,32,128]{2,1,0:T(8,128)}, u32[]{:S(2)}) copy-start(s32[7,32,128]{2,1,0:T(8,128)} %param.10) | copy-start | bytes 344068
  3.4 0.9 %copy-start.5 = (bf16[7,32,2,128]{3,2,1,0:T(2,128)(2,1)S(1)}, bf16[7,32,2,128]{3,2,1,0:T(2,128)(2,1)}, u32[]{:S(2)}) copy-start(bf16[7,32,2,128]{3,2,1,0:T(2,128)(2,1)} %param.9) | copy-start | bytes 344068
  4.3 1.2 %copy-start = (bf16[7,32,16,128]{3,2,1,0:T(8,128)(2,1)S(1)}, bf16[7,32,16,128]{3,2,1,0:T(8,128)(2,1)}, u32[]{:S(2)}) copy-start(bf16[7,32,16,128]{3,2,1,0:T(8,128)(2,1)} %innov_ref.1) | copy-start | bytes 2752516
  4.9 0.9 %copy-start.1 = (f32[4,32,128]{2,1,0:T(8,128)S(1)}, f32[4,32,128]{2,1,0:T(8,128)}, u32[]{:S(2)}) copy-start(f32[4,32,128]{2,1,0:T(8,128)} %u_ref.1) | copy-start | bytes 196612
  4.9 0.9 %copy-start.2 = (f32[4,32,128]{2,1,0:T(8,128)S(1)}, f32[4,32,128]{2,1,0:T(8,128)}, u32[]{:S(2)}) copy-start(f32[4,32,128]{2,1,0:T(8,128)} %v_ref.1) | copy-start | bytes 196612
  5.0 0.9 %copy-start.3 = (f32[16,16]{1,0:T(8,128)S(1)}, f32[16,16]{1,0:T(8,128)}, u32[]{:S(2)}) copy-start(f32[16,16]{1,0:T(8,128)} %mix_ref.1) | copy-start | bytes 3076
